TPU v7x, 32 devices: a whole 2x2x4 slice. The times are simulated.
32 devices in a mesh: dp: 16 (over z, x, core), tensor: 2 (over y).
Axes of the slice: x: 2, y: 2, z: 4, core: 2. Of those that a mesh axis runs over, the one named last changes fastest.
Arguments:
- target_tokens: bfloat16 [16, 1024, 768], P('dp'), may hold values from -6 to 6
- memory_tokens: bfloat16 [16, 1024, 768], P('dp'), may hold values from -6 to 6
- output_grad: bfloat16 [16, 1024, 768], P('dp'), may hold values from -6 to 6
- target_segments: int32 [16, 1024], P('dp'), may hold values from 0 to 3, as said below
- memory_segments: int32 [16, 1024], P('dp'), may hold values from 0 to 3, as said below
- norm1_gain: float32 [768], replicated, may hold values from 0.25 to 1.75
- norm1_shift: float32 [768], replicated, may hold values from -1.5 to 1.5
- self_query: bfloat16 [768, 768], P(None, 'tensor'), may hold values from -0.21875 to 0.21875
- self_key: bfloat16 [768, 768], P(None, 'tensor'), may hold values from -0.21875 to 0.21875
- self_value: bfloat16 [768, 768], P(None, 'tensor'), may hold values from -0.21875 to 0.21875
- self_out: bfloat16 [768, 768], P('tensor'), may hold values from -0.875 to 0.875
- norm2_gain: float32 [768], replicated, may hold values from 0.25 to 1.75
- norm2_shift: float32 [768], replicated, may hold values from -1.5 to 1.5
- cross_query: bfloat16 [768, 768], P(None, 'tensor'), may hold values from -0.21875 to 0.21875
- cross_key: bfloat16 [768, 768], P(None, 'tensor'), may hold values from -0.21875 to 0.21875
- cross_value: bfloat16 [768, 768], P(None, 'tensor'), may hold values from -0.21875 to 0.21875
- cross_out: bfloat16 [768, 768], P('tensor'), may hold values from -0.875 to 0.875
- norm3_gain: float32 [768], replicated, may hold values from 0.25 to 1.75
- norm3_shift: float32 [768], replicated, may hold values from -1.5 to 1.5
- ffn_up: bfloat16 [768, 3072], P(None, 'tensor'), may hold values from -0.21875 to 0.21875
- ffn_down: bfloat16 [3072, 768], P('tensor'), may hold values from -0.109375 to 0.109375
Outputs:
- layer_output: bfloat16 [16, 1024, 768], P('dp', 'tensor')
- input_grad: float32 [16, 1024, 768], P('dp', 'tensor')
- memory_grad: float32 [16, 1024, 768], P('dp', 'tensor')
- self_query_grad: float32 [768, 768], P('dp', 'tensor')
- self_key_grad: float32 [768, 768], P('dp', 'tensor')
- self_value_grad: float32 [768, 768], P('dp', 'tensor')
- self_out_grad: float32 [768, 768], P('tensor', 'dp')
- cross_query_grad: float32 [768, 768], P('dp', 'tensor')
- cross_key_grad: float32 [768, 768], P('dp', 'tensor')
- cross_value_grad: float32 [768, 768], P('dp', 'tensor')
- cross_out_grad: float32 [768, 768], P('tensor', 'dp')
- ffn_up_grad: float32 [768, 3072], P('dp', 'tensor')
- ffn_down_grad: float32 [3072, 768], P('tensor', 'dp')
- norm1_gain_grad: float32 [768], replicated
- norm1_shift_grad: float32 [768], replicated
- norm2_gain_grad: float32 [768], replicated
- norm2_shift_grad: float32 [768], replicated
- norm3_gain_grad: float32 [768], replicated
- norm3_shift_grad: float32 [768], replicated
Inputs may be any that keep to these rules, and one draw needn't show every extreme that they name: `target_segments`: per sequence the ids never fall, start at 0, and every id 0 to 3 occurs. `memory_segments`: per sequence the ids never fall, start at 0, and every id 0 to 3 occurs, so every target position has memory positions of its document.
All inputs are finite; a program needn't handle non-finite values.
Results may differ from a plain program's by a relative error of at most 0.028.
Values may be sent and summed in bfloat16 or wider, within the bound.
No kernel may reach another device: no remote copies, remote signals or barrier semaphores. Data moves between devices by JAX's collectives and lax.ppermute only.
A program may use at most 192 MiB of HBM per device.

v0:
```python
from functools import partial

import jax
import jax.numpy as jnp
from jax import lax
from jax.experimental import pallas as pl
from jax.experimental.pallas import tpu as pltpu
from jax.sharding import PartitionSpec as P

HEAD_DIM = 64
DOCS = 4
BLOCK = 256
LOW = -1e30
F32 = jnp.float32
BF16 = jnp.bfloat16
MIB = 1024 * 1024


def dot(left, right):
    return jnp.dot(left, right, preferred_element_type=F32)


def dot_nt(left, right):
    return lax.dot_general(left, right, (((1,), (1,)), ((), ())), preferred_element_type=F32)


def dot_tn(left, right):
    return lax.dot_general(left, right, (((0,), (0,)), ((), ())), preferred_element_type=F32)


def normalise(values):
    centered = values - jnp.mean(values, -1, keepdims=True)
    rstd = lax.rsqrt(jnp.mean(centered * centered, -1, keepdims=True) + 1e-05)
    return centered * rstd, rstd


def norm_backward(unit, rstd, gain, cotangent):
    scaled = cotangent * gain
    return rstd * (
        scaled
        - jnp.mean(scaled, -1, keepdims=True)
        - unit * jnp.mean(scaled * unit, -1, keepdims=True)
    )


def call(kernel, out_shape, *, flops, bytes_accessed, limit=16, scratch=(), scalars=1):
    def run(*operands):
        whole = pl.BlockSpec(memory_space=pltpu.VMEM)
        small = pl.BlockSpec(memory_space=pltpu.SMEM)
        return pl.pallas_call(
            kernel,
            out_shape=out_shape,
            in_specs=[small] * scalars + [whole] * (len(operands) - scalars),
            out_specs=jax.tree.map(lambda _: whole, out_shape),
            scratch_shapes=scratch,
            compiler_params=pltpu.CompilerParams(vmem_limit_bytes=limit * MIB),
            cost_estimate=pl.CostEstimate(
                flops=int(flops), bytes_accessed=int(bytes_accessed), transcendentals=0
            ),
        )(*operands)

    return run


def shape(dims, dtype):
    return jax.ShapeDtypeStruct(dims, dtype)


def full_spec(dims):
    return pl.BlockSpec(dims, lambda *_: (0,) * len(dims))


def row_blocks(rows):
    return [slice(first, first + BLOCK) for first in range(0, rows, BLOCK)]


def own_half(side, rows, first=0, count=None):
    count = rows if count is None else count
    return pl.ds(pl.multiple_of(side * rows + first, BLOCK), count)


def vector(ref, number):
    return ref[number : number + 1, :]


def norm_project_kernel(where_ref, x_ref, norms_ref, wq_ref, wkv_ref, a_ref, q_ref, kv_ref):
    for at in row_blocks(x_ref.shape[0]):
        unit, _ = normalise(x_ref[at].astype(F32))
        a_ref[at] = (unit * vector(norms_ref, 0) + vector(norms_ref, 1)).astype(BF16)
    rows = q_ref.shape[0]
    q_ref[...] = dot(a_ref[own_half(where_ref[0], rows), :], wq_ref[...]).astype(BF16)
    for at in row_blocks(x_ref.shape[0]):
        kv_ref[at] = dot(a_ref[at], wkv_ref[...]).astype(BF16)


def norm_project(side, x, norms, wq, wkv):
    rows, width = x.shape
    cols = wq.shape[1]
    return call(
        norm_project_kernel,
        (shape((rows, width), BF16), shape((rows // 2, cols), BF16), shape((rows, 2 * cols), BF16)),
        flops=5 * rows * width * cols,
        bytes_accessed=4 * rows * width,
    )(side, x, norms, wq, wkv)


def project_kernel(where_ref, a_ref, wq_ref, wkv_ref, q_ref, kv_ref):
    q_ref[...] = dot(a_ref[own_half(where_ref[0], q_ref.shape[0]), :], wq_ref[...]).astype(BF16)
    for at in row_blocks(a_ref.shape[0]):
        kv_ref[at] = dot(a_ref[at], wkv_ref[...]).astype(BF16)


def project(side, a, wq, wkv):
    rows, width = a.shape
    cols = wq.shape[1]
    return call(
        project_kernel,
        (shape((rows // 2, cols), BF16), shape((rows, 2 * cols), BF16)),
        flops=5 * rows * width * cols,
        bytes_accessed=4 * rows * width,
    )(side, a, wq, wkv)


def project_memory_kernel(a_ref, wkv_ref, kv_ref):
    for at in row_blocks(a_ref.shape[0]):
        kv_ref[at] = dot(a_ref[at], wkv_ref[...]).astype(BF16)


def project_memory(memory, wkv):
    rows, width = memory.shape
    return call(
        project_memory_kernel,
        shape((rows, wkv.shape[1]), BF16),
        flops=2 * rows * width * wkv.shape[1],
        bytes_accessed=4 * rows * width,
        scalars=0,
    )(memory, wkv)


def first_doc(starts_ref, row):
    doc = 0
    for number in range(1, DOCS):
        doc = doc + (starts_ref[0, number] <= row).astype(jnp.int32)
    return doc


def key_range(starts_ref, block_number, causal):
    first = block_number * BLOCK
    low = starts_ref[1, first_doc(starts_ref, first)]
    if causal:
        return low // BLOCK, block_number
    high = starts_ref[1, first_doc(starts_ref, first + BLOCK - 1) + 1]
    return low // BLOCK, (high + BLOCK - 1) // BLOCK


def lanes(rows):
    return lax.broadcasted_iota(jnp.int32, (rows, 128), 1)


def causal_mask():
    keys = lax.broadcasted_iota(jnp.int32, (BLOCK, BLOCK), 0)
    rows = lax.broadcasted_iota(jnp.int32, (BLOCK, BLOCK), 1)
    return keys <= rows


def pair_of(ref, pair, rows=slice(None)):
    return ref[rows, pair * 128 : (pair + 1) * 128]


def half_of(head):
    return slice(64 * (head % 2), 64 * (head % 2) + 64)


def in_three(value, place, otherwise):
    high = value.astype(BF16)
    rest = value - high.astype(F32)
    middle = rest.astype(BF16)
    low = (rest - middle.astype(F32)).astype(BF16)
    return jnp.where(place == 4, high, jnp.where(place == 5, middle, jnp.where(place == 6, low, otherwise)))


def walk_keys(starts_ref, block_number, causal, one_block):
    low, high = key_range(starts_ref, block_number, causal)
    if causal:
        one_block(block_number, causal_mask())
    lax.fori_loop(low, high, lambda number, _: (one_block(number, None), 0)[1], 0)


def attend_kernel(
    causal, heads, group, where_ref, starts_ref, q_ref, kv_ref, docs_ref, dock_ref, o_ref, qa_ref,
    ka_ref, vt_ref, qs_ref, acc_ref, max_ref,
):
    keys = kv_ref.shape[0]
    pairs = heads // 2
    left = lanes(keys) < 64
    for pair in range(pairs):
        turned = pair_of(kv_ref, pairs + pair).T
        for head in (2 * pair, 2 * pair + 1):
            mine = left if head % 2 == 0 else ~left
            ka_ref[head] = jnp.where(mine, pair_of(kv_ref, pair), dock_ref[...])
            vt_ref[head, :64] = turned[half_of(head)]
            vt_ref[head, 64:] = jnp.ones((16, keys), BF16)
    left = lanes(BLOCK) < 64
    place = lanes(BLOCK) % 64

    def one_step(step, _):
        at_rows = pl.ds(pl.multiple_of(step * BLOCK, BLOCK), BLOCK)
        block_number = where_ref[0] * (q_ref.shape[0] // BLOCK) + step
        docs = docs_ref[pl.ds(pl.multiple_of(block_number * BLOCK, BLOCK), BLOCK), :]
        for head in range(heads):
            mine = left if head % 2 == 0 else ~left
            scaled = pair_of(q_ref, head // 2, at_rows) * jnp.array(HEAD_DIM**-0.5, BF16)
            qs_ref[head] = jnp.where(mine, scaled, docs)
        max_ref[...] = jnp.full_like(max_ref, LOW)
        acc_ref[...] = jnp.zeros_like(acc_ref)

        def one_block(number, mask):
            at = pl.ds(pl.multiple_of(number * BLOCK, BLOCK), BLOCK)
            for first in range(0, heads, group):
                some = range(first, first + group)
                scores = [dot_nt(ka_ref[head, at, :], qs_ref[head]) for head in some]
                if mask is not None:
                    scores = [jnp.where(mask, score, LOW) for score in scores]
                old = [max_ref[head, 0:1] for head in some]
                new = [jnp.maximum(m, jnp.max(score, 0, keepdims=True)) for m, score in zip(old, scores)]
                weights = [jnp.exp(score - m).astype(BF16) for score, m in zip(scores, new)]
                mixed = [dot(vt_ref[head, :, at], weight) for head, weight in zip(some, weights)]
                shrink = [jnp.exp(m - n) for m, n in zip(old, new)]
                for number_in, head in enumerate(some):
                    acc_ref[head] = acc_ref[head] * shrink[number_in] + mixed[number_in]
                    max_ref[head, 0:1] = new[number_in]

        walk_keys(starts_ref, block_number, causal, one_block)
        for pair in range(pairs):
            both = []
            for head in (2 * pair, 2 * pair + 1):
                mine = left if head % 2 == 0 else ~left
                acc = acc_ref[head]
                total = acc[64:65]
                both.append(acc[:64] / total)
                lse = max_ref[head, 0:1] + jnp.log(total)
                column = jnp.broadcast_to(-lse, (128, BLOCK)).T
                qa_ref[head, at_rows, :] = jnp.where(mine, qs_ref[head], in_three(column, place, docs))
            o_ref[at_rows, pair * 128 : (pair + 1) * 128] = jnp.concatenate(both, 0).T.astype(BF16)
        return 0

    lax.fori_loop(0, q_ref.shape[0] // BLOCK, one_step, 0)


def attend(side, starts, q, kv, doc_rows, doc_keys, causal):
    rows, cols = q.shape
    heads = cols // HEAD_DIM
    keys = kv.shape[0]
    return call(
        partial(attend_kernel, causal, heads, heads),
        (shape((rows, cols), BF16), shape((heads, rows, 128), BF16)),
        flops=16 * rows * keys * cols,
        bytes_accessed=8 * keys * cols,
        scalars=2,
        limit=20,
        scratch=[
            pltpu.VMEM((heads, keys, 128), BF16),
            pltpu.VMEM((heads, 80, keys), BF16),
            pltpu.VMEM((heads, BLOCK, 128), BF16),
            pltpu.VMEM((heads, 80, BLOCK), F32),
            pltpu.VMEM((heads, 8, BLOCK), F32),
        ],
    )(side, starts, q, kv, doc_rows, doc_keys)


def attend_back_kernel(
    causal, heads, group, where_ref, starts_ref, qa_ref, kv_ref, do_ref, o_ref, dock_ref, dq_ref, dkv_ref,
    ka_ref, va_ref, da_ref, dqa_ref, dka_ref, dva_ref, kt_ref, qt_ref, dt_ref,
):
    keys = kv_ref.shape[0]
    pairs = heads // 2
    left = lanes(keys) < 64
    place = lanes(keys) % 64
    ones = jnp.where((place >= 4) & (place < 7), 1.0, 0.0).astype(BF16)
    for head in range(heads):
        mine = left if head % 2 == 0 else ~left
        ka_ref[head] = jnp.where(mine, pair_of(kv_ref, head // 2), dock_ref[...] + ones)
        va_ref[head] = jnp.where(mine, pair_of(kv_ref, pairs + head // 2), ones)
    for pair in range(pairs):
        kt_ref[pair] = pair_of(kv_ref, pair).T
    dka_ref[...] = jnp.zeros_like(dka_ref)
    dva_ref[...] = jnp.zeros_like(dva_ref)
    left = lanes(BLOCK) < 64
    place = lanes(BLOCK) % 64

    def one_step(step, _):
        at_rows = pl.ds(pl.multiple_of(step * BLOCK, BLOCK), BLOCK)
        block_number = where_ref[0] * (do_ref.shape[0] // BLOCK) + step
        for pair in range(pairs):
            grad = pair_of(do_ref, pair, at_rows)
            dt_ref[pair] = grad.T
            product = grad.astype(F32) * pair_of(o_ref, pair, at_rows).astype(F32)
            for head in (2 * pair, 2 * pair + 1):
                mine = left if head % 2 == 0 else ~left
                delta = -jnp.sum(jnp.where(mine, product, 0.0), -1, keepdims=True)
                delta = jnp.broadcast_to(delta, (BLOCK, 128))
                da_ref[head] = jnp.where(mine, grad, in_three(delta, place, jnp.zeros((), BF16)))
            qt_ref[pair] = jnp.where(left, qa_ref[2 * pair, at_rows, :], qa_ref[2 * pair + 1, at_rows, :]).T
        dqa_ref[...] = jnp.zeros_like(dqa_ref)

        def one_block(number, mask):
            at = pl.ds(pl.multiple_of(number * BLOCK, BLOCK), BLOCK)
            for first in range(0, heads, group):
                some = range(first, first + group)
                scores = [dot_nt(ka_ref[head, at, :], qa_ref[head, at_rows, :]) for head in some]
                grads = [dot_nt(va_ref[head, at, :], da_ref[head]) for head in some]
                if mask is not None:
                    scores = [jnp.where(mask, score, LOW) for score in scores]
                weights = [jnp.exp(score) for score in scores]
                grads = [(weight * grad).astype(BF16) for weight, grad in zip(weights, grads)]
                weights = [weight.astype(BF16) for weight in weights]
                values = [dot_nt(dt_ref[head // 2, half_of(head)], weight) for head, weight in zip(some, weights)]
                kept = [dot_nt(qt_ref[head // 2, half_of(head)], grad) for head, grad in zip(some, grads)]
                asked = [dot(kt_ref[head // 2, half_of(head), at], grad) for head, grad in zip(some, grads)]
                for number_in, head in enumerate(some):
                    dva_ref[head // 2, half_of(head), at] += values[number_in]
                    dka_ref[head // 2, half_of(head), at] += kept[number_in]
                    dqa_ref[head // 2, half_of(head)] += asked[number_in]

        walk_keys(starts_ref, block_number, causal, one_block)
        for pair in range(pairs):
            dq_ref[at_rows, pair * 128 : (pair + 1) * 128] = (dqa_ref[pair].T * HEAD_DIM**-0.5).astype(BF16)
        return 0

    lax.fori_loop(0, do_ref.shape[0] // BLOCK, one_step, 0)
    for pair in range(pairs):
        dkv_ref[:, pair * 128 : (pair + 1) * 128] = dka_ref[pair].astype(BF16).T
        dkv_ref[:, (pairs + pair) * 128 : (pairs + pair + 1) * 128] = dva_ref[pair].astype(BF16).T


def attend_back(side, starts, qa, kv, do, o, doc_keys, causal):
    rows, cols = do.shape
    heads = cols // HEAD_DIM
    keys = kv.shape[0]
    return call(
        partial(attend_back_kernel, causal, heads, heads // 2),
        (shape((rows, cols), BF16), shape((keys, 2 * cols), BF16)),
        flops=40 * rows * keys * cols,
        bytes_accessed=12 * keys * cols,
        scalars=2,
        limit=24,
        scratch=[
            pltpu.VMEM((heads, keys, 128), BF16),
            pltpu.VMEM((heads, keys, 128), BF16),
            pltpu.VMEM((heads, BLOCK, 128), BF16),
            pltpu.VMEM((heads // 2, 128, BLOCK), F32),
            pltpu.VMEM((heads // 2, 128, keys), F32),
            pltpu.VMEM((heads // 2, 128, keys), F32),
            pltpu.VMEM((heads // 2, 128, keys), BF16),
            pltpu.VMEM((heads // 2, 128, BLOCK), BF16),
            pltpu.VMEM((heads // 2, 128, BLOCK), BF16),
        ],
    )(side, starts, qa, kv, do, o, doc_keys)


def out_project(own, other, own_ref, other_ref):
    half = own_ref.shape[1]
    left = dot(own, own_ref[:half]) + dot(other, other_ref[:half])
    right = dot(own, own_ref[half:]) + dot(other, other_ref[half:])
    return jnp.concatenate([left, right], axis=1)


def after_self_kernel(where_ref, x_ref, own_ref, other_ref, wo_ref, wp_ref, norms_ref, wq_ref, wr_ref, s_ref, a_ref, q_ref, r_ref):
    rows = s_ref.shape[0]
    for at in row_blocks(rows):
        start = x_ref[own_half(where_ref[0], rows, at.start, BLOCK), :].astype(F32)
        stream = start + out_project(own_ref[at], other_ref[at], wo_ref, wp_ref)
        s_ref[at] = stream
        unit, _ = normalise(stream)
        a_ref[at] = (unit * vector(norms_ref, 2) + vector(norms_ref, 3)).astype(BF16)
    q_ref[...] = dot(a_ref[...], wq_ref[...]).astype(BF16)
    r_ref[...] = dot(a_ref[...], wr_ref[...]).astype(BF16)


def after_self(side, x, own, other, wo, wp, norms, wq, wr):
    rows, cols = own.shape
    width = x.shape[1]
    return call(
        after_self_kernel,
        (shape((rows, width), F32), shape((rows, width), BF16)) + (shape((rows, cols), BF16),) * 2,
        flops=8 * rows * width * cols,
        bytes_accessed=12 * rows * width,
    )(side, x, own, other, wo, wp, norms, wq, wr)


def after_cross_kernel(s_ref, own_ref, other_ref, wo_ref, wp_ref, norms_ref, t_ref, a_ref):
    for at in row_blocks(s_ref.shape[0]):
        stream = s_ref[at] + out_project(own_ref[at], other_ref[at], wo_ref, wp_ref)
        t_ref[at] = stream
        unit, _ = normalise(stream)
        a_ref[at] = (unit * vector(norms_ref, 4) + vector(norms_ref, 5)).astype(BF16)


def after_cross(stream, own, other, wo, wp, norms):
    rows, cols = own.shape
    width = stream.shape[1]
    return call(
        after_cross_kernel,
        (shape((rows, width), F32), shape((rows, width), BF16)),
        flops=4 * rows * width * cols,
        bytes_accessed=12 * rows * width,
        scalars=0,
    )(stream, own, other, wo, wp, norms)


def feed_kernel(where_ref, a_ref, e_ref, up_ref, down_ref, h_ref, du_ref, out_ref, r_ref, out_acc, r_acc):
    step = pl.program_id(0)

    @pl.when(step == 0)
    def _():
        out_acc[...] = jnp.zeros_like(out_acc)
        r_acc[...] = jnp.zeros_like(r_acc)

    rows = a_ref.shape[0]
    for at in row_blocks(rows):
        u = dot(a_ref[at], up_ref[...])
        dh = dot_nt(e_ref[own_half(where_ref[0], rows, at.start, BLOCK), :], down_ref[...])
        square = u * u
        curve = jnp.tanh(u * (0.7978845608028654 + 0.035677408136300125 * square))
        half = 0.5 + 0.5 * curve
        slope = half + (0.5 * u) * (1.0 - curve * curve) * (0.7978845608028654 + 0.10703222440890037 * square)
        h_ref[at] = (u * half).astype(BF16)
        du_ref[at] = (dh * slope).astype(BF16)
    out_acc[...] += dot(h_ref[...], down_ref[...])
    r_acc[...] += dot_nt(du_ref[...], up_ref[...])

    @pl.when(step == pl.num_programs(0) - 1)
    def _():
        out_ref[...] = out_acc[...].astype(out_ref.dtype)
        r_ref[...] = r_acc[...].astype(r_ref.dtype)


def feed(where, a, e, up, down, dtype, chunk=512):
    rows, width = a.shape
    hidden = up.shape[1]
    whole = full_spec((rows, width))
    return pl.pallas_call(
        feed_kernel,
        out_shape=(shape((rows, hidden), BF16),) * 2 + (shape((rows, width), dtype),) * 2,
        grid=(hidden // chunk,),
        in_specs=[
            pl.BlockSpec(memory_space=pltpu.SMEM), whole, full_spec(e.shape),
            pl.BlockSpec((width, chunk), lambda i: (0, i)), pl.BlockSpec((chunk, width), lambda i: (i, 0)),
        ],
        out_specs=(pl.BlockSpec((rows, chunk), lambda i: (0, i)),) * 2 + (whole,) * 2,
        scratch_shapes=[pltpu.VMEM((rows, width), F32)] * 2,
        compiler_params=pltpu.CompilerParams(vmem_limit_bytes=28 * MIB),
        cost_estimate=pl.CostEstimate(
            flops=8 * rows * width * hidden, bytes_accessed=4 * hidden * width, transcendentals=0
        ),
    )(where, a, e, up, down)


def grad_into_heads(e, weight_ref):
    half = weight_ref.shape[1]
    return (dot_nt(e[:, :half], weight_ref[:half]) + dot_nt(e[:, half:], weight_ref[half:])).astype(BF16)


def add_rows(ref, number, value):
    ref[number : number + 1, :] += jnp.sum(value, 0, keepdims=True)


def after_feed_kernel(where_ref, s_ref, r_ref, recv_ref, e_ref, norms_ref, wo_ref, wp_ref, g_ref, eb_ref, own_ref, other_ref, d_ref):
    rows = s_ref.shape[0]
    d_ref[...] = jnp.zeros_like(d_ref)
    for at in row_blocks(rows):
        unit, rstd = normalise(s_ref[at])
        cotangent = r_ref[at] + recv_ref[at].astype(F32)
        add_rows(d_ref, 0, cotangent * unit)
        add_rows(d_ref, 1, cotangent)
        top = e_ref[own_half(where_ref[0], rows, at.start, BLOCK), :].astype(F32)
        grad = top + norm_backward(unit, rstd, vector(norms_ref, 4), cotangent)
        g_ref[at] = grad
        eb_ref[at] = grad.astype(BF16)
    own_ref[...] = grad_into_heads(eb_ref[...], wo_ref)
    other_ref[...] = grad_into_heads(eb_ref[...], wp_ref)


def after_feed(side, stream, kept, received, e, norms, wo, wp):
    rows, width = stream.shape
    cols = wo.shape[1]
    return call(
        after_feed_kernel,
        (shape((rows, width), F32), shape((rows, width), BF16)) + (shape((rows, cols), BF16),) * 2
        + (shape((2, width), F32),),
        flops=4 * rows * width * cols,
        bytes_accessed=16 * rows * width,
        limit=20,
    )(side, stream, kept, received, e, norms, wo, wp)


def after_cross_back_kernel(
    s_ref, g_ref, dq_ref, dr_ref, wq_ref, wr_ref, norms_ref, wo_ref, wp_ref, out_ref, eb_ref, own_ref, other_ref, d_ref
):
    d_ref[...] = jnp.zeros_like(d_ref)
    for at in row_blocks(s_ref.shape[0]):
        unit, rstd = normalise(s_ref[at])
        cotangent = dot_nt(dq_ref[at], wq_ref[...]) + dot_nt(dr_ref[at], wr_ref[...])
        add_rows(d_ref, 0, cotangent * unit)
        add_rows(d_ref, 1, cotangent)
        grad = g_ref[at] + norm_backward(unit, rstd, vector(norms_ref, 2), cotangent)
        out_ref[at] = grad
        eb_ref[at] = grad.astype(BF16)
    own_ref[...] = grad_into_heads(eb_ref[...], wo_ref)
    other_ref[...] = grad_into_heads(eb_ref[...], wp_ref)


def after_cross_back(stream, grad, dq, dr, wq, wr, norms, wo, wp):
    rows, width = stream.shape
    cols = wo.shape[1]
    return call(
        after_cross_back_kernel,
        (shape((rows, width), F32), shape((rows, width), BF16)) + (shape((rows, cols), BF16),) * 2
        + (shape((2, width), F32),),
        flops=8 * rows * width * cols,
        bytes_accessed=16 * rows * width,
        scalars=0,
        limit=20,
    )(stream, grad, dq, dr, wq, wr, norms, wo, wp)


def key_value_back_kernel(with_queries, where_ref, own_ref, other_ref, wkv_ref, wlw_ref, *refs):
    if with_queries:
        dq_ref, dr_ref, wq_ref, wr_ref, x_ref, send_ref, keep_ref, d_ref = refs
        d_ref[...] = jnp.zeros_like(d_ref)
    else:
        send_ref, keep_ref = refs
    rows = send_ref.shape[0]
    side = where_ref[0]
    for half, target in ((1 - side, send_ref), (side, keep_ref)):
        for at in row_blocks(rows):
            place = own_half(half, rows, at.start, BLOCK)
            total = dot_nt(own_ref[place, :], wkv_ref[...]) + dot_nt(other_ref[place, :], wlw_ref[...])
            if with_queries:
                if target is keep_ref:
                    total += dot_nt(dq_ref[at], wq_ref[...]) + dot_nt(dr_ref[at], wr_ref[...])
                unit, _ = normalise(x_ref[place, :].astype(F32))
                add_rows(d_ref, 0, total * unit)
                add_rows(d_ref, 1, total)
            target[at] = total.astype(target.dtype)


def key_value_back(side, own, other, wkv, wlw, queries=()):
    rows = own.shape[0] // 2
    width = wkv.shape[0]
    cols = wkv.shape[1] // 2
    outs = (shape((rows, width), BF16), shape((rows, width), F32))
    if queries:
        outs += (shape((2, width), F32),)
    return call(
        partial(key_value_back_kernel, len(queries) > 0),
        outs,
        flops=18 * rows * width * cols,
        bytes_accessed=12 * rows * width,
        limit=20,
    )(side, own, other, wkv, wlw, *queries)


def input_grad_kernel(where_ref, x_ref, g_ref, keep_ref, recv_ref, norms_ref, out_ref):
    rows = g_ref.shape[0]
    for at in row_blocks(rows):
        unit, rstd = normalise(x_ref[own_half(where_ref[0], rows, at.start, BLOCK), :].astype(F32))
        cotangent = keep_ref[at] + recv_ref[at].astype(F32)
        out_ref[at] = g_ref[at] + norm_backward(unit, rstd, vector(norms_ref, 0), cotangent)


def input_grad(side, x, grad, kept, received, norms):
    rows, width = grad.shape
    return call(
        input_grad_kernel,
        shape((rows, width), F32),
        flops=rows * width * 20,
        bytes_accessed=16 * rows * width,
    )(side, x, grad, kept, received, norms)


def bit_reversed(number, bits):
    turned = 0
    for bit in range(bits):
        turned |= ((number >> bit) & 1) << (bits - 1 - bit)
    return turned


def store_parts(product, keep, send, core, parts):
    bits = parts.bit_length() - 1
    rows = product.shape[0] // parts
    product = product.astype(BF16)

    def write(target, wanted):
        for number in range(parts // 2):
            block = bit_reversed(number, bits - 1) * 2 + wanted
            target(number * rows, rows, product[block * rows : (block + 1) * rows])

    for value in (0, 1):
        @pl.when(core == value)
        def _():
            write(keep, value)
            write(send, 1 - value)


def put_columns(ref, columns):
    def put(first, count, value):
        ref[first : first + count, columns] = value

    return put


def attention_grads_kernel(parts, where_ref, wide_ref, a_ref, e_ref, dq_ref, dkv_ref, o_ref, keep_ref, send_ref):
    core = where_ref[0]
    cols = dq_ref.shape[1]
    narrow = a_ref[own_half(where_ref[1], dq_ref.shape[0]), :] if a_ref.shape[0] != dq_ref.shape[0] else a_ref[...]
    first = 0
    for left, right in ((narrow, dq_ref), (wide_ref[...], dkv_ref), (e_ref[...], o_ref)):
        columns = slice(first, first + right.shape[1])
        first += right.shape[1]
        product = dot_tn(left, right[...])
        store_parts(product, put_columns(keep_ref, columns), put_columns(send_ref, columns), core, parts)


def attention_grads(core_side, parts, wide, a, e, dq, dkv, o):
    rows, width = e.shape
    cols = dq.shape[1]
    out = shape((width // 2, 4 * cols), BF16)
    return call(
        partial(attention_grads_kernel, parts),
        (out, out),
        flops=2 * width * cols * (2 * rows + 2 * wide.shape[0]),
        bytes_accessed=6e6,
        limit=20,
    )(core_side, wide, a, e, dq, dkv, o)


def feed_grads_kernel(parts, half, where_ref, a0, a1, e_ref, du0, du1, h0, h1, keep_ref, send_ref):
    step = pl.program_id(0)
    core = where_ref[0]
    rows = a0.shape[0]
    put_keep = put_columns(keep_ref, slice(None))
    put_send = put_columns(send_ref, slice(None))

    @pl.when(step < half)
    def _():
        product = dot_tn(a0[...], du0[...]) + dot_tn(a1[...], du1[...])
        store_parts(product, put_keep, put_send, core, parts)

    @pl.when(step >= half)
    def _():
        mine = e_ref[own_half(where_ref[1], rows), :]
        theirs = e_ref[own_half(1 - where_ref[1], rows), :]
        product = dot_tn(mine, h0[...]) + dot_tn(theirs, h1[...])
        store_parts(product, put_keep, put_send, core, parts)


def feed_grads(where, parts, a0, a1, e, du0, du1, h0, h1, chunk=768):
    rows, width = a0.shape
    hidden = du0.shape[1]
    half = hidden // chunk
    out = shape((width // 2, 2 * hidden), BF16)
    first = pl.BlockSpec((rows, chunk), lambda i: (0, jnp.minimum(i, half - 1)))
    second = pl.BlockSpec((rows, chunk), lambda i: (0, jnp.maximum(i - half, 0)))
    return pl.pallas_call(
        partial(feed_grads_kernel, parts, half),
        out_shape=(out, out),
        grid=(2 * half,),
        in_specs=[pl.BlockSpec(memory_space=pltpu.SMEM)] + [full_spec((rows, width))] * 2 + [full_spec((2 * rows, width))]
        + [first] * 2 + [second] * 2,
        out_specs=(pl.BlockSpec((width // 2, chunk), lambda i: (0, i)),) * 2,
        compiler_params=pltpu.CompilerParams(vmem_limit_bytes=28 * MIB),
        cost_estimate=pl.CostEstimate(
            flops=8 * rows * width * hidden, bytes_accessed=16 * MIB, transcendentals=0
        ),
    )(where, a0, a1, e, du0, du1, h0, h1)


def swap_tensor(value):
    return lax.ppermute(value, "tensor", [(0, 1), (1, 0)])


def swap_dp(value, bit):
    count = lax.axis_size("dp")
    return lax.ppermute(value, "dp", [(number, number ^ (1 << bit)) for number in range(count)])


def after(value, *others):
    return lax.optimization_barrier((value,) + others)[0]


def share_group(first, part):
    second = swap_dp(first, 1)
    third = swap_dp(first, 0)
    fourth = swap_dp(second, 0)
    pieces = (first, third, second, fourth)
    q, k, v, o = (lax.select_n(part ^ number, *pieces) for number in range(4))
    return q, jnp.concatenate([k, v], axis=1), o


def halve(value, bit, place, axis=0):
    length = value.shape[axis] // 2
    mine = (place >> bit) & 1
    sent = lax.dynamic_slice_in_dim(value, (1 - mine) * length, length, axis)
    kept = lax.dynamic_slice_in_dim(value, mine * length, length, axis)
    return add(kept, swap_dp(sent, bit))


def add(left, right):
    return (left.astype(F32) + right.astype(F32)).astype(BF16)


def shards(
    target_tokens, memory_tokens, output_grad, target_segments, memory_segments,
    norm1_gain, norm1_shift, self_query, self_key, self_value, self_out,
    norm2_gain, norm2_shift, cross_query, cross_key, cross_value, cross_out,
    norm3_gain, norm3_shift, ffn_up, ffn_down,
):
    _, length, width = target_tokens.shape
    cols = self_query.shape[1]
    parts = lax.axis_size("dp")
    bits = parts.bit_length() - 1
    place = lax.axis_index("dp")
    side = lax.axis_index("tensor")
    core = place & 1
    x = target_tokens[0]
    memory = memory_tokens[0]
    e3 = output_grad[0]
    norms = jnp.stack([norm1_gain, norm1_shift, norm2_gain, norm2_shift, norm3_gain, norm3_shift])
    side_one = side.astype(jnp.int32).reshape(1)
    core_side = jnp.stack([core, side]).astype(jnp.int32)

    def folded(weight):
        return jnp.concatenate([weight[:, :cols], weight[:, cols:]], axis=0)

    part = place % 4
    self_wo = folded(self_out)
    cross_wo = folded(cross_out)
    self_first = swap_tensor(lax.select_n(part, self_query, self_key, self_value, self_wo))
    cross_sent = lax.select_n(part, cross_query, cross_key, cross_value, cross_wo)
    cross_first = swap_tensor(after(cross_sent, self_first))
    self_wq2, self_wkv2, self_wo2 = share_group(self_first, part)
    self_wkv = jnp.concatenate([self_key, self_value], axis=1)
    cross_wkv = jnp.concatenate([cross_key, cross_value], axis=1)

    numbers = jnp.arange(DOCS + 1)[:, None]
    target_starts = jnp.sum(target_segments < numbers, 1).astype(jnp.int32)
    memory_starts = jnp.sum(memory_segments < numbers, 1).astype(jnp.int32)
    self_starts = jnp.stack([target_starts, target_starts])
    cross_starts = jnp.stack([target_starts, memory_starts])
    lane = jnp.arange(128) % 64
    hot = target_segments[0][:, None] == lane[None, :]
    doc_rows = jnp.where(hot, LOW, 0.0).astype(BF16)
    doc_target = jnp.where((lane < DOCS)[None, :] & ~hot, 1.0, 0.0).astype(BF16)
    doc_memory = jnp.where(
        (lane < DOCS)[None, :] & (memory_segments[0][:, None] != lane[None, :]), 1.0, 0.0
    ).astype(BF16)

    a1, q_own, kv_own = norm_project(side_one, x, norms, self_query, self_wkv)
    o1_own, qa1_own = attend(side_one, self_starts, q_own, kv_own, doc_rows, doc_target, True)
    kv2_own = project_memory(memory, cross_wkv)
    q_oth, kv_oth = project(side_one, after(a1, o1_own, kv2_own), self_wq2, self_wkv2)
    o1_oth, qa1_oth = attend(side_one, self_starts, q_oth, kv_oth, doc_rows, doc_target, True)
    cross_wq2, cross_wkv2, cross_wo2 = share_group(after(cross_first, q_oth), part)
    stream1, a2, q2_own, q2_oth = after_self(
        side_one, x, o1_own, o1_oth, self_wo, self_wo2, norms, cross_query, cross_wq2
    )
    o2_own, qa2_own = attend(side_one, cross_starts, q2_own, kv2_own, doc_rows, doc_memory, False)
    kv2_oth = project_memory(memory, cross_wkv2)
    o2_oth, qa2_oth = attend(side_one, cross_starts, q2_oth, kv2_oth, doc_rows, doc_memory, False)
    stream2, a3 = after_cross(stream1, o2_own, o2_oth, cross_wo, cross_wo2, norms)

    a3_oth = swap_tensor(a3)
    h_own, du_own, out_own, r3_own = feed(side_one, a3, e3, ffn_up, ffn_down, F32)
    a3_oth = after(a3_oth, r3_own)
    h_oth, du_oth, out_oth, r3_oth = feed(1 - side_one, a3_oth, e3, ffn_up, ffn_down, BF16)
    r3_recv = swap_tensor(r3_oth)
    aligned = (width // parts) % 16 == 0
    static_parts = parts if aligned else 2
    keep_f, send_f = feed_grads(core_side, static_parts, a3, a3_oth, e3, du_own, du_oth, h_own, h_oth)
    r3_recv = after(r3_recv, keep_f)
    out_recv = swap_tensor(after(out_oth, r3_recv))

    def reordered(keep, send):
        if aligned:
            return keep, send
        whole = jnp.where(core == 0, jnp.concatenate([keep, send]), jnp.concatenate([send, keep]))
        order = [bit_reversed(number, bits) for number in range(parts)]
        whole = jnp.take(whole.reshape(parts, width // parts, -1), jnp.array(order), axis=0)
        whole = whole.reshape(2, width // 2, -1)
        pick = lambda index: lax.dynamic_index_in_dim(whole, index, 0, False)
        return pick(core), pick(1 - core)

    def reduce_core(keep, send):
        keep, send = reordered(keep, send)
        return add(keep, swap_dp(send, 0))

    sum_f = reduce_core(keep_f, send_f)
    grad2, e2, do2_own, do2_oth, d3 = after_feed(side_one, stream2, r3_own, r3_recv, e3, norms, cross_wo, cross_wo2)
    do2_own = after(do2_own, sum_f)
    sum_f = halve(sum_f, 1, place)
    dq2_own, dkv2_own = attend_back(side_one, cross_starts, qa2_own, kv2_own, do2_own, o2_own, doc_memory, False)
    do2_oth = after(do2_oth, dq2_own)
    dq2_oth, dkv2_oth = attend_back(side_one, cross_starts, qa2_oth, kv2_oth, do2_oth, o2_oth, doc_memory, False)
    keep_c, send_c = attention_grads(core_side, static_parts, memory, a2, e2, dq2_own, dkv2_own, o2_own)
    keep_d, send_d = attention_grads(core_side, static_parts, memory, a2, e2, dq2_oth, dkv2_oth, o2_oth)
    dq2_oth = after(dq2_oth, sum_f, keep_c, keep_d)
    if bits > 2:
        sum_f = halve(sum_f, 2, place)
    sum_c = reduce_core(keep_c, send_c)
    sum_d = reduce_core(keep_d, send_d)
    grad1, e1, do1_own, do1_oth, d2 = after_cross_back(
        stream1, grad2, dq2_own, dq2_oth, cross_query, cross_wq2, norms, self_wo, self_wo2
    )
    send_m, keep_m = key_value_back(side_one, dkv2_own, after(dkv2_oth, grad1), cross_wkv, cross_wkv2)
    grad_memory = keep_m + swap_tensor(send_m).astype(F32)
    layer_output = (stream2 + out_own + after(out_recv, grad1).astype(F32)).astype(BF16)

    do1_own = after(do1_own, sum_f, sum_c, sum_d, send_m, layer_output)
    for bit in range(3, bits):
        sum_f = halve(sum_f, bit, place)
    sum_cd = halve(jnp.stack([sum_c, sum_d]), 1, place, 1)
    dq1_own, dkv1_own = attend_back(side_one, self_starts, qa1_own, kv_own, do1_own, o1_own, doc_target, True)
    keep_s, send_s = attention_grads(core_side, static_parts, a1, a1, e1, dq1_own, dkv1_own, o1_own)
    sum_s = reduce_core(keep_s, send_s)
    do1_oth = after(do1_oth, keep_s, sum_f)
    dq1_oth, dkv1_oth = attend_back(side_one, self_starts, qa1_oth, kv_oth, do1_oth, o1_oth, doc_target, True)
    dq1_oth = after(dq1_oth, sum_s, sum_cd)
    sum_s = halve(sum_s, 1, place)
    send_r, keep_r, d1 = key_value_back(
        side_one, dkv1_own, dkv1_oth, self_wkv, self_wkv2, (dq1_own, dq1_oth, self_query, self_wq2, x)
    )
    recv_r = swap_tensor(send_r)
    keep_t, send_t = attention_grads(core_side, static_parts, a1, a1, e1, after(dq1_oth, send_r), dkv1_oth, o1_oth)
    sum_t = reduce_core(keep_t, send_t)
    grad_x = input_grad(side_one, x, grad1, keep_r, recv_r, norms)
    sum_c = add(sum_cd[0], swap_tensor(after(sum_cd[1], recv_r)))
    sum_t = halve(sum_t, 1, place)
    sum_s = add(sum_s, swap_tensor(sum_t))
    for bit in range(2, bits):
        sum_c = halve(sum_c, bit, place)
        sum_s = halve(sum_s, bit, place)

    small = jnp.concatenate([d1, d2, d3], axis=0)
    small = small + swap_tensor(small)
    for bit in range(bits):
        small = small + swap_dp(small, bit)

    def four(total):
        pieces = [total[:, number * cols : (number + 1) * cols].astype(F32) for number in range(4)]
        return tuple(pieces[:3]) + (pieces[3].T,)

    hidden = ffn_up.shape[1]
    return (
        (layer_output[None], grad_x[None], grad_memory[None])
        + four(sum_s)
        + four(sum_c)
        + (sum_f[:, :hidden].astype(F32), sum_f[:, hidden:].astype(F32).T)
        + tuple(small[number] for number in range(6))
    )


def solution(mesh):
    tokens = P("dp", None, None)
    columns = P(None, "tensor")
    rows = P("tensor", None)
    block = (P(), P(), columns, columns, columns, rows)
    in_specs = (tokens,) * 3 + (P("dp", None),) * 2 + block + block + (P(), P(), columns, rows)
    out_rows = P("dp", "tensor")
    out_cols = P("tensor", "dp")
    four = (out_rows, out_rows, out_rows, out_cols)
    out_specs = (P("dp", "tensor", None),) * 3 + four + four + (out_rows, out_cols) + (P(),) * 6
    return jax.shard_map(shards, mesh=mesh, in_specs=in_specs, out_specs=out_specs, check_vma=False)
```

profile of v0, /device:TPU:0, one launch (start us, length us, event | category | flops | bytes accessed | tf_op | source)
XLA Modules:
  0.0 340.0 jit_solution(16349858964357746481)
XLA Ops:
  11.9 9.5 %collective-permute-done = bf16[768,384]{1,0:T(8,128)(2,1)} collective-permute-done((bf16[768,384]{1,0:T(8,128)(2,1)}, bf16[768,384]{1,0:T(8,128)(2,1)}, u32[]{:S(2)}, u32[]{:S(2)}) %collective-permute-start) | collective-permute-done | bytes 589856 | tf_op jit(solution)/shard_map/ppermute | solution.py:680
  31.5 4.7 %collective-permute-done.2 = bf16[768,384]{1,0:T(8,128)(2,1)} collective-permute-done((bf16[768,384]{1,0:T(8,128)(2,1)}, bf16[768,384]{1,0:T(8,128)(2,1)}, u32[]{:S(2)}, u32[]{:S(2)}) %collective-permute-start.2) | collective-permute-done | bytes 589856 | tf_op jit(solution)/shard_map/ppermute | solution.py:685
  38.1 4.4 %shard_map.349 = (bf16[512,384]{1,0:T(8,128)(2,1)S(1)}, bf16[6,512,128]{2,1,0:T(8,128)(2,1)S(1)}) custom-call(s32[1]{0:T(128)} %bitcast.where_ref, s32[2,5]{1,0:T(2,128)S(1)} %get-tuple-element.209.starts_ref, bf16[512,384]{1,0:T(8,128)(2,1)S(1)} %get-tuple-element.95.q_ref, bf16[1024,768]{1,0:T(8,128)(2,1)S(1)} %copy-done.66, ...), custom_call_target="tpu_custom_call" | custom-call | flops 3221225472 | bytes 3145728 | tf_op jit(solution)/shard_map/pallas_call | solution.py:50
  42.5 4.4 %collective-permute-start.4 = (bf16[768,384]{1,0:T(8,128)(2,1)S(1)}, bf16[768,384]{1,0:T(8,128)(2,1)S(1)}, u32[]{:S(2)}, u32[]{:S(2)}) collective-permute-start(bf16[768,384]{1,0:T(8,128)(2,1)S(1)} %copy-done.80), channel_id=1, source_target_pairs={{0,1},{1,0},{2,3},{3,2},{4,5},{5,4},{6,7},{7,6},{8,9},{9,8},{10,11... | collective-permute-start | bytes 1769480 | tf_op jit(solution)/shard_map/ppermute | solution.py:680
  52.7 6.0 %collective-permute-done.4 = bf16[768,384]{1,0:T(8,128)(2,1)S(1)} collective-permute-done((bf16[768,384]{1,0:T(8,128)(2,1)S(1)}, bf16[768,384]{1,0:T(8,128)(2,1)S(1)}, u32[]{:S(2)}, u32[]{:S(2)}) %collective-permute-start.4) | collective-permute-done | bytes 589856 | tf_op jit(solution)/shard_map/ppermute | solution.py:680
  60.0 13.8 %collective-permute-done.6 = bf16[768,384]{1,0:T(8,128)(2,1)S(1)} collective-permute-done((bf16[768,384]{1,0:T(8,128)(2,1)S(1)}, bf16[768,384]{1,0:T(8,128)(2,1)S(1)}, u32[]{:S(2)}, u32[]{:S(2)}) %collective-permute-start.6) | collective-permute-done | bytes 589856 | tf_op jit(solution)/shard_map/ppermute | solution.py:685
  73.8 4.2 %shard_map.352 = (bf16[512,384]{1,0:T(8,128)(2,1)S(1)}, bf16[6,512,128]{2,1,0:T(8,128)(2,1)S(1)}) custom-call(s32[1]{0:T(128)} %bitcast.where_ref, s32[2,5]{1,0:T(2,128)S(1)} %get-tuple-element.209.starts_ref, bf16[512,384]{1,0:T(8,128)(2,1)S(1)} %get-tuple-element.100.q_ref, bf16[1024,768]{1,0:T(8,128)(2,1)S(1)} %get-tuple-element.101.kv_ref, ...), custom_call_target="tpu_custom_call" | custom-call | flops 3221225472 | bytes 3145728 | tf_op jit(solution)/shard_map/pallas_call | solution.py:50
  86.1 5.1 %shard_map.354 = (bf16[512,384]{1,0:T(8,128)(2,1)S(1)}, bf16[6,512,128]{2,1,0:T(8,128)(2,1)S(1)}) custom-call(s32[1]{0:T(128)} %bitcast.where_ref, s32[2,5]{1,0:T(2,128)S(1)} %get-tuple-element.208.starts_ref, bf16[512,384]{1,0:T(8,128)(2,1)S(1)} %get-tuple-element.106.q_ref, bf16[1024,768]{1,0:T(8,128)(2,1)S(1)} %copy-done.58, ...), custom_call_target="tpu_custom_call" | custom-call | flops 3221225472 | bytes 3145728 | tf_op jit(solution)/shard_map/pallas_call | solution.py:50
  92.1 5.5 %shard_map.356 = (bf16[512,384]{1,0:T(8,128)(2,1)S(1)}, bf16[6,512,128]{2,1,0:T(8,128)(2,1)S(1)}) custom-call(s32[1]{0:T(128)} %bitcast.where_ref, s32[2,5]{1,0:T(2,128)S(1)} %get-tuple-element.208.starts_ref, bf16[512,384]{1,0:T(8,128)(2,1)S(1)} %get-tuple-element.108.q_ref, bf16[1024,768]{1,0:T(8,128)(2,1)S(1)} %shard_map.355.kv_ref, ...), custom_call_target="tpu_custom_call" | custom-call | flops 3221225472 | bytes 3145728 | tf_op jit(solution)/shard_map/pallas_call | solution.py:50
  101.2 7.9 %collective-permute-start.8 = (bf16[512,768]{1,0:T(8,128)(2,1)}, bf16[512,768]{1,0:T(8,128)(2,1)}, u32[]{:S(2)}, u32[]{:S(2)}) collective-permute-start(bf16[512,768]{1,0:T(8,128)(2,1)} %get-tuple-element.111.a_ref.a0), channel_id=1, source_target_pairs={{0,1},{1,0},{2,3},{3,2},{4,5},{5,4},{6,7},{7,6},{8,9},{9,8},{10,11... | collective-permute-start | bytes 2359304 | tf_op jit(solution)/shard_map/ppermute | solution.py:680
  113.9 7.9 %shard_map.358 = (bf16[512,1536]{1,0:T(8,128)(2,1)S(1)}, bf16[512,1536]{1,0:T(8,128)(2,1)S(1)}, f32[512,768]{1,0:T(8,128)S(1)}, f32[512,768]{1,0:T(8,128)S(1)}) custom-call(s32[1]{0:T(128)} %bitcast.where_ref, bf16[512,768]{1,0:T(8,128)(2,1)} %get-tuple-element.111.a_ref.a0, bf16[1024,768]{1,0:T(8,128)(2,1)S(1)} %bitcast.32, ...), custom_call_target="tpu_custom_call" | custom-call | flops 4831838208 | bytes 4718592 | tf_op jit(solution)/shard_map/pallas_call | solution.py:442
  125.9 8.8 %shard_map.359 = (bf16[512,1536]{1,0:T(8,128)(2,1)S(1)}, bf16[512,1536]{1,0:T(8,128)(2,1)S(1)}, bf16[512,768]{1,0:T(8,128)(2,1)S(1)}, bf16[512,768]{1,0:T(8,128)(2,1)}) custom-call(s32[1]{0:T(128)S(6)} %sub.8.where_ref, bf16[512,768]{1,0:T(8,128)(2,1)} %collective-permute-done.8.a_ref.a1, bf16[1024,768]{1,0:T(8,128)(2,1)S(1)} %bitcast.33, ...), custom_call_target="tpu_custom_call" | custom-call | flops 4831838208 | bytes 4718592 | tf_op jit(solution)/shard_map/pallas_call | solution.py:442
  135.6 9.2 %shard_map.360 = (bf16[384,3072]{1,0:T(8,128)(2,1)S(1)}, bf16[384,3072]{1,0:T(8,128)(2,1)}) custom-call(s32[2]{0:T(128)S(1)} %pad_add_fusion.2.where_ref, bf16[512,768]{1,0:T(8,128)(2,1)} %get-tuple-element.111.a_ref.a0, bf16[512,768]{1,0:T(8,128)(2,1)} %collective-permute-done.8.a_ref.a1, bf16[1024,768]{1,0:T(8,128)(2,1)S(1)} %bitcast.34, ...), custom_call_target="tpu_custom_call" | custom-call | flops 4831838208 | bytes 16777216 | tf_op jit(solution)/shard_map/pallas_call | solution.py:665
  146.5 20.0 %collective-permute-done.9.recv_ref = bf16[512,768]{1,0:T(8,128)(2,1)} collective-permute-done((bf16[512,768]{1,0:T(8,128)(2,1)}, bf16[512,768]{1,0:T(8,128)(2,1)}, u32[]{:S(2)}, u32[]{:S(2)}) %collective-permute-start.9) | collective-permute-done | bytes 786464 | tf_op jit(solution)/shard_map/ppermute | solution.py:680
  181.0 7.8 %shard_map.362 = (bf16[512,384]{1,0:T(8,128)(2,1)S(1)}, bf16[1024,768]{1,0:T(8,128)(2,1)S(1)}) custom-call(s32[1]{0:T(128)} %bitcast.where_ref, s32[2,5]{1,0:T(2,128)S(1)} %get-tuple-element.208.starts_ref, bf16[6,512,128]{2,1,0:T(8,128)(2,1)S(1)} %copy-done.77, bf16[1024,768]{1,0:T(8,128)(2,1)S(1)} %copy-done.59, ...), custom_call_target="tpu_custom_call" | custom-call | flops 8053063680 | bytes 4718592 | tf_op jit(solution)/shard_map/pallas_call | solution.py:50
  188.9 4.3 %shard_map.364 = (bf16[384,1536]{1,0:T(8,128)(2,1)S(1)}, bf16[384,1536]{1,0:T(8,128)(2,1)S(1)}) custom-call(s32[2]{0:T(128)S(1)} %pad_add_fusion.2.where_ref, bf16[1024,768]{1,0:T(8,128)(2,1)S(1)} %bitcast.38, bf16[512,768]{1,0:T(8,128)(2,1)S(1)} %copy-done.55, bf16[512,768]{1,0:T(8,128)(2,1)S(1)} %get-tuple-element.135.e_ref, ...), custom_call_target="tpu_custom_call" | custom-call | flops 1811939328 | bytes 6000000 | tf_op jit(solution)/shard_map/pallas_call | solution.py:50
  196.1 7.8 %shard_map.363 = (bf16[512,384]{1,0:T(8,128)(2,1)S(1)}, bf16[1024,768]{1,0:T(8,128)(2,1)S(1)}) custom-call(s32[1]{0:T(128)} %bitcast.where_ref, s32[2,5]{1,0:T(2,128)S(1)} %get-tuple-element.208.starts_ref, bf16[6,512,128]{2,1,0:T(8,128)(2,1)S(1)} %copy-done.75, bf16[1024,768]{1,0:T(8,128)(2,1)S(1)} %copy-done.61, ...), custom_call_target="tpu_custom_call" | custom-call | flops 8053063680 | bytes 4718592 | tf_op jit(solution)/shard_map/pallas_call | solution.py:50
  203.9 4.7 %shard_map.365 = (bf16[384,1536]{1,0:T(8,128)(2,1)S(1)}, bf16[384,1536]{1,0:T(8,128)(2,1)S(1)}) custom-call(s32[2]{0:T(128)S(1)} %pad_add_fusion.2.where_ref, bf16[1024,768]{1,0:T(8,128)(2,1)S(1)} %bitcast.39, bf16[512,768]{1,0:T(8,128)(2,1)S(1)} %copy-done.55, bf16[512,768]{1,0:T(8,128)(2,1)S(1)} %get-tuple-element.135.e_ref, ...), custom_call_target="tpu_custom_call" | custom-call | flops 1811939328 | bytes 6000000 | tf_op jit(solution)/shard_map/pallas_call | solution.py:50
  220.7 4.4 %collective-permute-start.20 = (bf16[512,768]{1,0:T(8,128)(2,1)S(1)}, bf16[512,768]{1,0:T(8,128)(2,1)S(1)}, u32[]{:S(2)}, u32[]{:S(2)}) collective-permute-start(bf16[512,768]{1,0:T(8,128)(2,1)S(1)} %get-tuple-element.148), channel_id=1, source_target_pairs={{0,1},{1,0},{2,3},{3,2},{4,5},{5,4},{6,7},{7,6},{8,9},{9,8},{10,11... | collective-permute-start | bytes 2359304 | tf_op jit(solution)/shard_map/ppermute | solution.py:680
  226.4 5.1 %collective-permute-done.13 = bf16[96,3072]{1,0:T(8,128)(2,1)S(1)} collective-permute-done((bf16[96,3072]{1,0:T(8,128)(2,1)S(1)}, bf16[96,3072]{1,0:T(8,128)(2,1)S(1)}, u32[]{:S(2)}, u32[]{:S(2)}) %collective-permute-start.13) | collective-permute-done | bytes 589856 | tf_op jit(solution)/shard_map/ppermute | solution.py:685
  232.9 6.2 %shard_map.368 = (bf16[512,384]{1,0:T(8,128)(2,1)S(1)}, bf16[1024,768]{1,0:T(8,128)(2,1)S(1)}) custom-call(s32[1]{0:T(128)} %bitcast.where_ref, s32[2,5]{1,0:T(2,128)S(1)} %get-tuple-element.209.starts_ref, bf16[6,512,128]{2,1,0:T(8,128)(2,1)S(1)} %copy-done.71, bf16[1024,768]{1,0:T(8,128)(2,1)S(1)} %copy-done.67, ...), custom_call_target="tpu_custom_call" | custom-call | flops 8053063680 | bytes 4718592 | tf_op jit(solution)/shard_map/pallas_call | solution.py:50
  239.1 4.5 %shard_map.369 = (bf16[384,1536]{1,0:T(8,128)(2,1)S(1)}, bf16[384,1536]{1,0:T(8,128)(2,1)S(1)}) custom-call(s32[2]{0:T(128)S(1)} %pad_add_fusion.2.where_ref, bf16[1024,768]{1,0:T(8,128)(2,1)S(1)} %copy-done.64, bf16[1024,768]{1,0:T(8,128)(2,1)S(1)} %copy-done.64, bf16[512,768]{1,0:T(8,128)(2,1)S(1)} %get-tuple-element.153.e_ref, ...), custom_call_target="tpu_custom_call" | custom-call | flops 1811939328 | bytes 6000000 | tf_op jit(solution)/shard_map/pallas_call | solution.py:50
  243.7 4.3 %collective-permute-done.16 = bf16[48,3072]{1,0:T(8,128)(2,1)S(1)} collective-permute-done((bf16[48,3072]{1,0:T(8,128)(2,1)S(1)}, bf16[48,3072]{1,0:T(8,128)(2,1)S(1)}, u32[]{:S(2)}, u32[]{:S(2)}) %collective-permute-start.16) | collective-permute-done | bytes 294944 | tf_op jit(solution)/shard_map/ppermute | solution.py:685
  248.1 6.2 %shard_map.370 = (bf16[512,384]{1,0:T(8,128)(2,1)S(1)}, bf16[1024,768]{1,0:T(8,128)(2,1)S(1)}) custom-call(s32[1]{0:T(128)} %bitcast.where_ref, s32[2,5]{1,0:T(2,128)S(1)} %get-tuple-element.209.starts_ref, bf16[6,512,128]{2,1,0:T(8,128)(2,1)S(1)} %copy-done.73, bf16[1024,768]{1,0:T(8,128)(2,1)S(1)} %copy-done.69, ...), custom_call_target="tpu_custom_call" | custom-call | flops 8053063680 | bytes 4718592 | tf_op jit(solution)/shard_map/pallas_call | solution.py:50
  256.6 3.9 %shard_map.371 = (bf16[512,768]{1,0:T(8,128)(2,1)S(1)}, f32[512,768]{1,0:T(8,128)S(1)}, f32[2,768]{1,0:T(2,128)S(1)}) custom-call(s32[1]{0:T(128)} %bitcast.where_ref, bf16[1024,768]{1,0:T(8,128)(2,1)S(1)} %get-tuple-element.150.dkv_ref.own_ref, bf16[1024,768]{1,0:T(8,128)(2,1)S(1)} %get-tuple-element.157.other_ref.dkv_ref, bf16[768,768]{1,0:T(8,128)(2,1)S(1)} %copy-done.44, ...), custom_call_target="tpu_custom_call" | custom-call | flops 2717908992 | bytes 4718592 | tf_op jit(solution)/shard_map/pallas_call | solution.py:50
  260.5 3.8 %collective-permute-start.30 = (f32[6,768]{1,0:T(8,128)S(1)}, f32[6,768]{1,0:T(8,128)S(1)}, u32[]{:S(2)}, u32[]{:S(2)}) collective-permute-start(f32[6,768]{1,0:T(8,128)S(1)} %pad_maximum_fusion.4), channel_id=1, source_target_pairs={{0,1},{1,0},{2,3},{3,2},{4,5},{5,4},{6,7},{7,6},{8,9},{9,8},{10,11... | collective-permute-start | bytes 55304 | tf_op jit(solution)/shard_map/ppermute | solution.py:680
  266.2 4.5 %shard_map.373 = (bf16[384,1536]{1,0:T(8,128)(2,1)S(1)}, bf16[384,1536]{1,0:T(8,128)(2,1)S(1)}) custom-call(s32[2]{0:T(128)S(1)} %pad_add_fusion.2.where_ref, bf16[1024,768]{1,0:T(8,128)(2,1)S(1)} %copy-done.64, bf16[1024,768]{1,0:T(8,128)(2,1)S(1)} %copy-done.64, bf16[512,768]{1,0:T(8,128)(2,1)S(1)} %get-tuple-element.153.e_ref, ...), custom_call_target="tpu_custom_call" | custom-call | flops 1811939328 | bytes 6000000 | tf_op jit(solution)/shard_map/pallas_call | solution.py:50
  284.8 8.2 %collective-permute-done.19.recv_ref = bf16[512,768]{1,0:T(8,128)(2,1)S(1)} collective-permute-done((bf16[512,768]{1,0:T(8,128)(2,1)S(1)}, bf16[512,768]{1,0:T(8,128)(2,1)S(1)}, u32[]{:S(2)}, u32[]{:S(2)}) %collective-permute-start.19) | collective-permute-done | bytes 786464 | tf_op jit(solution)/shard_map/ppermute | solution.py:680
  298.1 9.2 %collective-permute-done.27 = bf16[192,1536]{1,0:T(8,128)(2,1)S(1)} collective-permute-done((bf16[192,1536]{1,0:T(8,128)(2,1)S(1)}, bf16[192,1536]{1,0:T(8,128)(2,1)S(1)}, u32[]{:S(2)}, u32[]{:S(2)}) %collective-permute-start.27) | collective-permute-done | bytes 589856 | tf_op jit(solution)/shard_map/ppermute | solution.py:680
  316.1 8.2 %collective-permute-done.24 = bf16[192,1536]{1,0:T(8,128)(2,1)S(1)} collective-permute-done((bf16[192,1536]{1,0:T(8,128)(2,1)S(1)}, bf16[192,1536]{1,0:T(8,128)(2,1)S(1)}, u32[]{:S(2)}, u32[]{:S(2)}) %collective-permute-start.24) | collective-permute-done | bytes 589856 | tf_op jit(solution)/shard_map/ppermute | solution.py:680
  324.7 7.4 %collective-permute-done.25 = bf16[96,1536]{1,0:T(8,128)(2,1)S(1)} collective-permute-done((bf16[96,1536]{1,0:T(8,128)(2,1)S(1)}, bf16[96,1536]{1,0:T(8,128)(2,1)S(1)}, u32[]{:S(2)}, u32[]{:S(2)}) %collective-permute-start.25) | collective-permute-done | bytes 294944 | tf_op jit(solution)/shard_map/ppermute | solution.py:685
  334.7 4.4 %collective-permute-done.26 = bf16[48,1536]{1,0:T(8,128)(2,1)S(1)} collective-permute-done((bf16[48,1536]{1,0:T(8,128)(2,1)S(1)}, bf16[48,1536]{1,0:T(8,128)(2,1)S(1)}, u32[]{:S(2)}, u32[]{:S(2)}) %collective-permute-start.26) | collective-permute-done | bytes 147488 | tf_op jit(solution)/shard_map/ppermute | solution.py:685
  (305 shorter events, 121.4 us)
Async XLA Ops:
  4.8 16.6 %collective-permute-start = (bf16[768,384]{1,0:T(8,128)(2,1)}, bf16[768,384]{1,0:T(8,128)(2,1)}, u32[]{:S(2)}, u32[]{:S(2)}) collective-permute-start(bf16[768,384]{1,0:T(8,128)(2,1)} %get-tuple-element.191), channel_id=1, source_target_pairs={{0,1},{1,0},{2,3},{3,2},{4,5},{5,4},{6,7},{7,6},{8,9},{9,8},{10,11... | collective-permute-start | bytes 1769480 | tf_op jit(solution)/shard_map/ppermute | solution.py:680
  21.4 14.8 %collective-permute-start.2 = (bf16[768,384]{1,0:T(8,128)(2,1)}, bf16[768,384]{1,0:T(8,128)(2,1)}, u32[]{:S(2)}, u32[]{:S(2)}) collective-permute-start(bf16[768,384]{1,0:T(8,128)(2,1)} %collective-permute-done), channel_id=1, source_target_pairs={{0,4},{2,6},{4,0},{6,2},{8,12},{10,14},{12,8},{14,10},{16,20},{18,... | collective-permute-start | bytes 1769480 | tf_op jit(solution)/shard_map/ppermute | solution.py:685
  31.5 15.5 %collective-permute-start.1 = (bf16[768,384]{1,0:T(8,128)(2,1)}, bf16[768,384]{1,0:T(8,128)(2,1)S(1)}, u32[]{:S(2)}, u32[]{:S(2)}) collective-permute-start(bf16[768,384]{1,0:T(8,128)(2,1)} %collective-permute-done), channel_id=1, source_target_pairs={{0,2},{2,0},{4,6},{6,4},{8,10},{10,8},{12,14},{14,12},{16,18},{18,... | collective-permute-start | bytes 1769480 | tf_op jit(solution)/shard_map/ppermute | solution.py:685
  36.2 10.7 %collective-permute-start.3 = (bf16[768,384]{1,0:T(8,128)(2,1)}, bf16[768,384]{1,0:T(8,128)(2,1)S(1)}, u32[]{:S(2)}, u32[]{:S(2)}) collective-permute-start(bf16[768,384]{1,0:T(8,128)(2,1)} %collective-permute-done.2), channel_id=1, source_target_pairs={{0,2},{2,0},{4,6},{6,4},{8,10},{10,8},{12,14},{14,12},{16,18},{18,... | collective-permute-start | bytes 1769480 | tf_op jit(solution)/shard_map/ppermute | solution.py:685
  42.5 16.2 %collective-permute-start.4 = (bf16[768,384]{1,0:T(8,128)(2,1)S(1)}, bf16[768,384]{1,0:T(8,128)(2,1)S(1)}, u32[]{:S(2)}, u32[]{:S(2)}) collective-permute-start(bf16[768,384]{1,0:T(8,128)(2,1)S(1)} %copy-done.80), channel_id=1, source_target_pairs={{0,1},{1,0},{2,3},{3,2},{4,5},{5,4},{6,7},{7,6},{8,9},{9,8},{10,11... | collective-permute-start | bytes 1769480 | tf_op jit(solution)/shard_map/ppermute | solution.py:680
  58.8 15.0 %collective-permute-start.6 = (bf16[768,384]{1,0:T(8,128)(2,1)S(1)}, bf16[768,384]{1,0:T(8,128)(2,1)S(1)}, u32[]{:S(2)}, u32[]{:S(2)}) collective-permute-start(bf16[768,384]{1,0:T(8,128)(2,1)S(1)} %collective-permute-done.4), channel_id=1, source_target_pairs={{0,4},{2,6},{4,0},{6,2},{8,12},{10,14},{12,8},{14,10},{16,20},{18,... | collective-permute-start | bytes 1769480 | tf_op jit(solution)/shard_map/ppermute | solution.py:685
  60.0 18.8 %collective-permute-start.5 = (bf16[768,384]{1,0:T(8,128)(2,1)S(1)}, bf16[768,384]{1,0:T(8,128)(2,1)S(1)}, u32[]{:S(2)}, u32[]{:S(2)}) collective-permute-start(bf16[768,384]{1,0:T(8,128)(2,1)S(1)} %collective-permute-done.4), channel_id=1, source_target_pairs={{0,2},{2,0},{4,6},{6,4},{8,10},{10,8},{12,14},{14,12},{16,18},{18,... | collective-permute-start | bytes 1769480 | tf_op jit(solution)/shard_map/ppermute | solution.py:685
  73.8 5.1 %collective-permute-start.7 = (bf16[768,384]{1,0:T(8,128)(2,1)S(1)}, bf16[768,384]{1,0:T(8,128)(2,1)S(1)}, u32[]{:S(2)}, u32[]{:S(2)}) collective-permute-start(bf16[768,384]{1,0:T(8,128)(2,1)S(1)} %collective-permute-done.6), channel_id=1, source_target_pairs={{0,2},{2,0},{4,6},{6,4},{8,10},{10,8},{12,14},{14,12},{16,18},{18,... | collective-permute-start | bytes 1769480 | tf_op jit(solution)/shard_map/ppermute | solution.py:685
  101.2 24.7 %collective-permute-start.8 = (bf16[512,768]{1,0:T(8,128)(2,1)}, bf16[512,768]{1,0:T(8,128)(2,1)}, u32[]{:S(2)}, u32[]{:S(2)}) collective-permute-start(bf16[512,768]{1,0:T(8,128)(2,1)} %get-tuple-element.111.a_ref.a0), channel_id=1, source_target_pairs={{0,1},{1,0},{2,3},{3,2},{4,5},{5,4},{6,7},{7,6},{8,9},{9,8},{10,11... | collective-permute-start | bytes 2359304 | tf_op jit(solution)/shard_map/ppermute | solution.py:680
  146.3 30.5 %collective-permute-start.11 = (bf16[384,3072]{1,0:T(8,128)(2,1)}, bf16[384,3072]{1,0:T(8,128)(2,1)}, u32[]{:S(2)}, u32[]{:S(2)}) collective-permute-start(bf16[384,3072]{1,0:T(8,128)(2,1)} %get-tuple-element.127), channel_id=1, source_target_pairs={{0,2},{2,0},{4,6},{6,4},{8,10},{10,8},{12,14},{14,12},{16,18},{18,... | collective-permute-start | bytes 7077896 | tf_op jit(solution)/shard_map/ppermute | solution.py:685
  146.3 20.3 %collective-permute-start.9 = (bf16[512,768]{1,0:T(8,128)(2,1)}, bf16[512,768]{1,0:T(8,128)(2,1)}, u32[]{:S(2)}, u32[]{:S(2)}) collective-permute-start(bf16[512,768]{1,0:T(8,128)(2,1)} %get-tuple-element.116), channel_id=1, source_target_pairs={{0,1},{1,0},{2,3},{3,2},{4,5},{5,4},{6,7},{7,6},{8,9},{9,8},{10,11... | collective-permute-start | bytes 2359304 | tf_op jit(solution)/shard_map/ppermute | solution.py:680
  166.5 48.7 %collective-permute-start.10 = (bf16[512,768]{1,0:T(8,128)(2,1)}, bf16[512,768]{1,0:T(8,128)(2,1)S(1)}, u32[]{:S(2)}, u32[]{:S(2)}) collective-permute-start(bf16[512,768]{1,0:T(8,128)(2,1)} %copy-done.56), channel_id=1, source_target_pairs={{0,1},{1,0},{2,3},{3,2},{4,5},{5,4},{6,7},{7,6},{8,9},{9,8},{10,11... | collective-permute-start | bytes 2359304 | tf_op jit(solution)/shard_map/ppermute | solution.py:680
  179.5 32.6 %collective-permute-start.12 = (bf16[192,3072]{1,0:T(8,128)(2,1)S(1)}, bf16[192,3072]{1,0:T(8,128)(2,1)S(1)}, u32[]{:S(2)}, u32[]{:S(2)}) collective-permute-start(bf16[192,3072]{1,0:T(8,128)(2,1)S(1)} %constant_dynamic-slice_fusion.8), channel_id=1, source_target_pairs={{0,4},{2,6},{4,0},{6,2},{8,12},{10,14},{12,8},{14,10},{16,20},{18,... | collective-permute-start | bytes 3538952 | tf_op jit(solution)/shard_map/ppermute | solution.py:685
  193.2 22.6 %collective-permute-start.14 = (bf16[384,1536]{1,0:T(8,128)(2,1)S(1)}, bf16[384,1536]{1,0:T(8,128)(2,1)S(1)}, u32[]{:S(2)}, u32[]{:S(2)}) collective-permute-start(bf16[384,1536]{1,0:T(8,128)(2,1)S(1)} %get-tuple-element.145), channel_id=1, source_target_pairs={{0,2},{2,0},{4,6},{6,4},{8,10},{10,8},{12,14},{14,12},{16,18},{18,... | collective-permute-start | bytes 3538952 | tf_op jit(solution)/shard_map/ppermute | solution.py:685
  208.7 7.5 %collective-permute-start.15 = (bf16[384,1536]{1,0:T(8,128)(2,1)S(1)}, bf16[384,1536]{1,0:T(8,128)(2,1)S(1)}, u32[]{:S(2)}, u32[]{:S(2)}) collective-permute-start(bf16[384,1536]{1,0:T(8,128)(2,1)S(1)} %get-tuple-element.146), channel_id=1, source_target_pairs={{0,2},{2,0},{4,6},{6,4},{8,10},{10,8},{12,14},{14,12},{16,18},{18,... | collective-permute-start | bytes 3538952 | tf_op jit(solution)/shard_map/ppermute | solution.py:685
  215.3 16.2 %collective-permute-start.13 = (bf16[96,3072]{1,0:T(8,128)(2,1)S(1)}, bf16[96,3072]{1,0:T(8,128)(2,1)S(1)}, u32[]{:S(2)}, u32[]{:S(2)}) collective-permute-start(bf16[96,3072]{1,0:T(8,128)(2,1)S(1)} %constant_dynamic-slice_fusion.7), channel_id=1, source_target_pairs={{0,8},{2,10},{4,12},{6,14},{8,0},{10,2},{12,4},{14,6},{16,24},{18,... | collective-permute-start | bytes 1769480 | tf_op jit(solution)/shard_map/ppermute | solution.py:685
  216.6 37.7 %collective-permute-start.18 = (bf16[2,192,1536]{2,1,0:T(8,128)(2,1)S(1)}, bf16[2,192,1536]{2,1,0:T(8,128)(2,1)S(1)}, u32[]{:S(2)}, u32[]{:S(2)}) collective-permute-start(bf16[2,192,1536]{2,1,0:T(8,128)(2,1)S(1)} %fusion), channel_id=1, source_target_pairs={{0,4},{2,6},{4,0},{6,2},{8,12},{10,14},{12,8},{14,10},{16,20},{18,... | collective-permute-start | bytes 3538952 | tf_op jit(solution)/shard_map/ppermute | solution.py:685
  220.7 43.6 %collective-permute-start.20 = (bf16[512,768]{1,0:T(8,128)(2,1)S(1)}, bf16[512,768]{1,0:T(8,128)(2,1)S(1)}, u32[]{:S(2)}, u32[]{:S(2)}) collective-permute-start(bf16[512,768]{1,0:T(8,128)(2,1)S(1)} %get-tuple-element.148), channel_id=1, source_target_pairs={{0,1},{1,0},{2,3},{3,2},{4,5},{5,4},{6,7},{7,6},{8,9},{9,8},{10,11... | collective-permute-start | bytes 2359304 | tf_op jit(solution)/shard_map/ppermute | solution.py:680
  231.7 16.3 %collective-permute-start.16 = (bf16[48,3072]{1,0:T(8,128)(2,1)S(1)}, bf16[48,3072]{1,0:T(8,128)(2,1)S(1)}, u32[]{:S(2)}, u32[]{:S(2)}) collective-permute-start(bf16[48,3072]{1,0:T(8,128)(2,1)S(1)} %constant_dynamic-slice_fusion.6), channel_id=1, source_target_pairs={{0,16},{2,18},{4,20},{6,22},{8,24},{10,26},{12,28},{14,30},{16,0},... | collective-permute-start | bytes 884744 | tf_op jit(solution)/shard_map/ppermute | solution.py:685
  243.6 11.1 %collective-permute-start.17 = (bf16[384,1536]{1,0:T(8,128)(2,1)S(1)}, bf16[384,1536]{1,0:T(8,128)(2,1)S(1)}, u32[]{:S(2)}, u32[]{:S(2)}) collective-permute-start(bf16[384,1536]{1,0:T(8,128)(2,1)S(1)} %get-tuple-element.159), channel_id=1, source_target_pairs={{0,2},{2,0},{4,6},{6,4},{8,10},{10,8},{12,14},{14,12},{16,18},{18,... | collective-permute-start | bytes 3538952 | tf_op jit(solution)/shard_map/ppermute | solution.py:685
  260.5 5.6 %collective-permute-start.30 = (f32[6,768]{1,0:T(8,128)S(1)}, f32[6,768]{1,0:T(8,128)S(1)}, u32[]{:S(2)}, u32[]{:S(2)}) collective-permute-start(f32[6,768]{1,0:T(8,128)S(1)} %pad_maximum_fusion.4), channel_id=1, source_target_pairs={{0,1},{1,0},{2,3},{3,2},{4,5},{5,4},{6,7},{7,6},{8,9},{9,8},{10,11... | collective-permute-start | bytes 55304 | tf_op jit(solution)/shard_map/ppermute | solution.py:680
  266.1 5.2 %collective-permute-start.31 = (f32[6,768]{1,0:T(8,128)S(1)}, f32[6,768]{1,0:T(8,128)S(1)}, u32[]{:S(2)}, u32[]{:S(2)}) collective-permute-start(f32[6,768]{1,0:T(8,128)S(1)} %fusion.5), channel_id=1, source_target_pairs={{0,2},{2,0},{4,6},{6,4},{8,10},{10,8},{12,14},{14,12},{16,18},{18,... | collective-permute-start | bytes 55304 | tf_op jit(solution)/shard_map/ppermute | solution.py:685
  270.8 26.2 %collective-permute-start.22 = (bf16[384,1536]{1,0:T(8,128)(2,1)S(1)}, bf16[384,1536]{1,0:T(8,128)(2,1)S(1)}, u32[]{:S(2)}, u32[]{:S(2)}) collective-permute-start(bf16[384,1536]{1,0:T(8,128)(2,1)S(1)} %get-tuple-element.166), channel_id=1, source_target_pairs={{0,2},{2,0},{4,6},{6,4},{8,10},{10,8},{12,14},{14,12},{16,18},{18,... | collective-permute-start | bytes 3538952 | tf_op jit(solution)/shard_map/ppermute | solution.py:685
  273.5 19.5 %collective-permute-start.19 = (bf16[512,768]{1,0:T(8,128)(2,1)S(1)}, bf16[512,768]{1,0:T(8,128)(2,1)S(1)}, u32[]{:S(2)}, u32[]{:S(2)}) collective-permute-start(bf16[512,768]{1,0:T(8,128)(2,1)S(1)} %get-tuple-element.162), channel_id=1, source_target_pairs={{0,1},{1,0},{2,3},{3,2},{4,5},{5,4},{6,7},{7,6},{8,9},{9,8},{10,11... | collective-permute-start | bytes 2359304 | tf_op jit(solution)/shard_map/ppermute | solution.py:680
  280.5 35.6 %collective-permute-start.21 = (bf16[192,1536]{1,0:T(8,128)(2,1)S(1)}, bf16[192,1536]{1,0:T(8,128)(2,1)S(1)}, u32[]{:S(2)}, u32[]{:S(2)}) collective-permute-start(bf16[192,1536]{1,0:T(8,128)(2,1)S(1)} %constant_dynamic-slice_fusion.5), channel_id=1, source_target_pairs={{0,4},{2,6},{4,0},{6,2},{8,12},{10,14},{12,8},{14,10},{16,20},{18,... | collective-permute-start | bytes 1769480 | tf_op jit(solution)/shard_map/ppermute | solution.py:685
  293.0 14.4 %collective-permute-start.27 = (bf16[192,1536]{1,0:T(8,128)(2,1)S(1)}, bf16[192,1536]{1,0:T(8,128)(2,1)S(1)}, u32[]{:S(2)}, u32[]{:S(2)}) collective-permute-start(bf16[192,1536]{1,0:T(8,128)(2,1)S(1)} %slice_bitcast_fusion), channel_id=1, source_target_pairs={{0,1},{1,0},{2,3},{3,2},{4,5},{5,4},{6,7},{7,6},{8,9},{9,8},{10,11... | collective-permute-start | bytes 1769480 | tf_op jit(solution)/shard_map/ppermute | solution.py:680
  297.3 13.9 %collective-permute-start.23 = (bf16[192,1536]{1,0:T(8,128)(2,1)S(1)}, bf16[192,1536]{1,0:T(8,128)(2,1)S(1)}, u32[]{:S(2)}, u32[]{:S(2)}) collective-permute-start(bf16[192,1536]{1,0:T(8,128)(2,1)S(1)} %constant_dynamic-slice_fusion.4), channel_id=1, source_target_pairs={{0,4},{2,6},{4,0},{6,2},{8,12},{10,14},{12,8},{14,10},{16,20},{18,... | collective-permute-start | bytes 1769480 | tf_op jit(solution)/shard_map/ppermute | solution.py:685
  307.6 7.2 %collective-permute-start.28 = (bf16[96,1536]{1,0:T(8,128)(2,1)S(1)}, bf16[96,1536]{1,0:T(8,128)(2,1)S(1)}, u32[]{:S(2)}, u32[]{:S(2)}) collective-permute-start(bf16[96,1536]{1,0:T(8,128)(2,1)S(1)} %constant_dynamic-slice_fusion.1), channel_id=1, source_target_pairs={{0,8},{2,10},{4,12},{6,14},{8,0},{10,2},{12,4},{14,6},{16,24},{18,... | collective-permute-start | bytes 884744 | tf_op jit(solution)/shard_map/ppermute | solution.py:685
  311.3 13.0 %collective-permute-start.24 = (bf16[192,1536]{1,0:T(8,128)(2,1)S(1)}, bf16[192,1536]{1,0:T(8,128)(2,1)S(1)}, u32[]{:S(2)}, u32[]{:S(2)}) collective-permute-start(bf16[192,1536]{1,0:T(8,128)(2,1)S(1)} %add_convert_fusion.9), channel_id=1, source_target_pairs={{0,1},{1,0},{2,3},{3,2},{4,5},{5,4},{6,7},{7,6},{8,9},{9,8},{10,11... | collective-permute-start | bytes 1769480 | tf_op jit(solution)/shard_map/ppermute | solution.py:680
  314.9 9.7 %collective-permute-start.29 = (bf16[48,1536]{1,0:T(8,128)(2,1)S(1)}, bf16[48,1536]{1,0:T(8,128)(2,1)S(1)}, u32[]{:S(2)}, u32[]{:S(2)}) collective-permute-start(bf16[48,1536]{1,0:T(8,128)(2,1)S(1)} %constant_dynamic-slice_fusion), channel_id=1, source_target_pairs={{0,16},{2,18},{4,20},{6,22},{8,24},{10,26},{12,28},{14,30},{16,0},... | collective-permute-start | bytes 442376 | tf_op jit(solution)/shard_map/ppermute | solution.py:685
  324.6 7.5 %collective-permute-start.25 = (bf16[96,1536]{1,0:T(8,128)(2,1)S(1)}, bf16[96,1536]{1,0:T(8,128)(2,1)S(1)}, u32[]{:S(2)}, u32[]{:S(2)}) collective-permute-start(bf16[96,1536]{1,0:T(8,128)(2,1)S(1)} %constant_dynamic-slice_fusion.3), channel_id=1, source_target_pairs={{0,8},{2,10},{4,12},{6,14},{8,0},{10,2},{12,4},{14,6},{16,24},{18,... | collective-permute-start | bytes 884744 | tf_op jit(solution)/shard_map/ppermute | solution.py:685
  332.2 6.9 %collective-permute-start.26 = (bf16[48,1536]{1,0:T(8,128)(2,1)S(1)}, bf16[48,1536]{1,0:T(8,128)(2,1)S(1)}, u32[]{:S(2)}, u32[]{:S(2)}) collective-permute-start(bf16[48,1536]{1,0:T(8,128)(2,1)S(1)} %constant_dynamic-slice_fusion.2), channel_id=1, source_target_pairs={{0,16},{2,18},{4,20},{6,22},{8,24},{10,26},{12,28},{14,30},{16,0},... | collective-permute-start | bytes 442376 | tf_op jit(solution)/shard_map/ppermute | solution.py:685
  (92 other events, 516.9 us)
where the time goes:
time: 346 us; the launch traced here: 340 us
  Pallas kernels  119 us (34%)
  waiting for transfers between devices  117 us (34%)
  starting transfers between devices  48.3 us (14%)
  local copies, waits for them, and re-layouts  35.2 us (10%)
  other arithmetic  18.6 us (5%)
    pallas_call x23, Pallas kernels, run(): pl.pallas_call(kernel, out_shape=out_shape, in_specs=[small] * scalars +...  92.7 us
    ppermute x10, waiting for transfers between devices, swap_tensor(): return lax.ppermute(value, 'tensor', [(0, 1), (1, 0)])  64.5 us
    ppermute x25, waiting for transfers between devices, swap_dp(): lax.ppermute(value, 'dp', [(number, number ^ 1 << bit) for number in rang...  52.5 us
    unnamed x178, local copies, waits for them, and re-layouts  31.6 us
    ppermute x10, starting transfers between devices, swap_tensor(): return lax.ppermute(value, 'tensor', [(0, 1), (1, 0)])  28.5 us
    ppermute x25, starting transfers between devices, swap_dp(): lax.ppermute(value, 'dp', [(number, number ^ 1 << bit) for number in rang...  19.8 us
    pallas_call x2, Pallas kernels, feed(): pl.pallas_call(feed_kernel, out_shape=(shape((rows, hidden), BF16),) * 2...  16.7 us
    pallas_call x1, Pallas kernels, feed_grads(): pl.pallas_call(partial(feed_grads_kernel, parts, half), out_shape=(out, o...  9.22 us
  transfers between devices with their start and end apart: 35, of which 18 were waited for; matrix products, arithmetic and copies ran while one was open for 5% of the time, Pallas kernels for 25%

commit v1 on v0

v1 whole, which is shorter than its diff:
```python
from functools import partial

import jax
import jax.numpy as jnp
from jax import lax
from jax.experimental import pallas as pl
from jax.experimental.pallas import tpu as pltpu
from jax.sharding import PartitionSpec as P

HEAD_DIM = 64
DOCS = 4
BLOCK = 256
LOW = -1e30
NORM_ROWS = 16
SPARE = 12
COST = 0.02
F32 = jnp.float32
BF16 = jnp.bfloat16
MIB = 1024 * 1024


def dot(left, right):
    return jnp.dot(left, right, preferred_element_type=F32)


def dot_nt(left, right):
    return lax.dot_general(left, right, (((1,), (1,)), ((), ())), preferred_element_type=F32)


def dot_tn(left, right):
    return lax.dot_general(left, right, (((0,), (0,)), ((), ())), preferred_element_type=F32)


def normalise(values):
    centered = values - jnp.mean(values, -1, keepdims=True)
    rstd = lax.rsqrt(jnp.mean(centered * centered, -1, keepdims=True) + 1e-05)
    return centered * rstd, rstd


def norm_backward(unit, rstd, gain, cotangent):
    scaled = cotangent * gain
    return rstd * (
        scaled
        - jnp.mean(scaled, -1, keepdims=True)
        - unit * jnp.mean(scaled * unit, -1, keepdims=True)
    )


PARTS = {"Q": (0, 1), "K": (1, 2), "O": (3, 1)}


class Staged:
    def __init__(self, arriving, leaving, spare):
        self.arriving, self.leaving, self.spare, self.sent = arriving, leaving, list(spare), []

    def need(self, *refs):
        for number, (ref, copy) in enumerate(self.arriving):
            if copy is not None and any(ref is wanted for wanted in refs):
                copy.wait()
                self.arriving[number] = (ref, None)

    def fetch(self, *refs):
        for ref, copy in self.arriving:
            if any(ref is wanted for wanted in refs):
                copy.start()

    def send(self, *refs):
        for number, (ref, target, sem) in enumerate(self.leaving):
            if target is not None and any(ref is wanted for wanted in refs):
                self.sent.append(pltpu.make_async_copy(ref, target, sem))
                self.sent[-1].start()
                self.leaving[number] = (ref, None, sem)

    def send_columns(self, refs, columns, last):
        for number, (ref, target, sem) in enumerate(self.leaving):
            if target is not None and any(ref is wanted for wanted in refs):
                if not last:
                    sem = self.spare.pop()
                self.sent.append(pltpu.make_async_copy(ref.at[:, columns], target.at[:, columns], sem))
                self.sent[-1].start()
                if last:
                    self.leaving[number] = (ref, None, sem)

    def finish(self):
        self.need(*(ref for ref, _ in self.arriving))
        self.send(*(ref for ref, _, _ in self.leaving))
        for copy in self.sent:
            copy.wait()


def call(kernel, out_shape, *, far="", far_out="", flops=0, limit=36, scratch=(), scalars=1):
    single = not isinstance(out_shape, tuple)
    shapes = (out_shape,) if single else out_shape

    def run(*operands):
        vmem = pl.BlockSpec(memory_space=pltpu.VMEM)
        hbm = pl.BlockSpec(memory_space=pltpu.HBM)
        small = pl.BlockSpec(memory_space=pltpu.SMEM)
        arrays = operands[scalars:]
        marks = far.ljust(len(arrays), "N")
        out_marks = far_out.ljust(len(shapes), "N")
        assert len(marks) == len(arrays) and len(out_marks) == len(shapes), (len(arrays), len(shapes))
        also = [number for number, mark in enumerate(out_marks) if mark == "B"]
        buffers, out_buffers = [], []
        for mark, array in zip(marks, arrays):
            dims = array.shape
            if mark == "H":
                dims = (dims[0] // 2,) + dims[1:]
            elif mark == "R":
                dims = (shapes[0].shape[0],) + dims[1:]
            elif mark in PARTS:
                dims = (dims[0], dims[1] // 4 * PARTS[mark][1])
            buffers.append(pltpu.VMEM(dims, array.dtype) if mark != "N" else None)
        for mark, item in zip(out_marks, shapes):
            out_buffers.append(pltpu.VMEM(item.shape, item.dtype) if mark == "F" else None)
        extra = [item for item in buffers + out_buffers if item is not None]
        copies = len(extra) + len(also)
        extra.append(pltpu.SemaphoreType.DMA((copies + SPARE,)))

        def wrapped(*refs):
            heads, refs = refs[:scalars], refs[scalars:]
            ins, refs = list(refs[: len(arrays)]), refs[len(arrays) :]
            outs, refs = list(refs[: len(shapes)]), refs[len(shapes) :]
            seconds, refs = refs[: len(also)], refs[len(also) :]
            own, refs = refs[: len(scratch)], refs[len(scratch) :]
            held, sems = list(refs[:-1]), refs[-1]
            arriving, leaving, place = [], [], 0
            for number, mark in enumerate(marks):
                if mark != "N":
                    source = ins[number]
                    if mark == "H":
                        rows = source.shape[0] // 2
                        source = source.at[pl.ds(pl.multiple_of(heads[0][0] * rows, BLOCK), rows)]
                    elif mark == "R":
                        source = source.at[pl.ds(pl.multiple_of(heads[0][0] * BLOCK, BLOCK), shapes[0].shape[0])]
                    elif mark in PARTS:
                        quarter = source.shape[1] // 4
                        source = source.at[:, pl.ds(PARTS[mark][0] * quarter, PARTS[mark][1] * quarter)]
                    ins[number] = held.pop(0)
                    copy = pltpu.make_async_copy(source, ins[number], sems.at[place])
                    if mark != "L":
                        copy.start()
                    arriving.append((ins[number], copy))
                    place += 1
            for number, mark in enumerate(out_marks):
                if mark == "F":
                    target, outs[number] = outs[number], held.pop(0)
                    leaving.append((outs[number], target, sems.at[place]))
                    place += 1
            for number, second in zip(also, seconds):
                leaving.append((outs[number], second, sems.at[place]))
                place += 1
            stage = Staged(arriving, leaving, [sems.at[copies + number] for number in range(SPARE)])
            kernel(stage, *heads, *ins, *outs, *own)
            stage.finish()

        kept = [pltpu.HBM(item.shape, item.dtype) if mark == "F" else item for item, mark in zip(shapes, out_marks)]
        kept += [pltpu.HBM(shapes[number].shape, shapes[number].dtype) for number in also]
        pinned = [
            pltpu.with_memory_space_constraint(array, pltpu.HBM) if mark != "N" else array
            for array, mark in zip(arrays, marks)
        ]
        results = pl.pallas_call(
            wrapped,
            out_shape=tuple(kept),
            in_specs=[small] * scalars + [vmem if mark == "N" else hbm for mark in marks],
            out_specs=tuple(hbm if mark == "F" else vmem for mark in out_marks) + (hbm,) * len(also),
            scratch_shapes=list(scratch) + extra,
            compiler_params=pltpu.CompilerParams(vmem_limit_bytes=limit * MIB),
            cost_estimate=pl.CostEstimate(flops=int(COST * flops), bytes_accessed=4096, transcendentals=0),
        )(*operands[:scalars], *pinned)
        return results[0] if len(results) == 1 else results

    return run


def shape(dims, dtype):
    return jax.ShapeDtypeStruct(dims, dtype)


def row_blocks(rows):
    return [slice(first, first + BLOCK) for first in range(0, rows, BLOCK)]


def own_half(side, rows, first=0, count=None):
    count = rows if count is None else count
    return pl.ds(pl.multiple_of(side * rows + first, BLOCK), count)


def vector(ref, number):
    return ref[number : number + 1, :]


def norm_project_kernel(stage, where_ref, x_ref, norms_ref, wq_ref, wkv_ref, a_ref, q_ref, kv_ref):
    stage.need(x_ref)
    for at in row_blocks(x_ref.shape[0]):
        unit, _ = normalise(x_ref[at].astype(F32))
        a_ref[at] = (unit * vector(norms_ref, 0) + vector(norms_ref, 1)).astype(BF16)
    stage.send(a_ref)
    rows = q_ref.shape[0]
    stage.need(wkv_ref)
    for at in row_blocks(x_ref.shape[0]):
        kv_ref[at] = dot(a_ref[at], wkv_ref[...]).astype(BF16)
    stage.send(kv_ref)
    stage.need(wq_ref)
    q_ref[...] = dot(a_ref[own_half(where_ref[0], rows), :], wq_ref[...]).astype(BF16)


def project_kernel(stage, where_ref, a_ref, wq_ref, wkv_ref, q_ref, kv_ref):
    stage.need(a_ref, wkv_ref)
    for at in row_blocks(a_ref.shape[0]):
        kv_ref[at] = dot(a_ref[at], wkv_ref[...]).astype(BF16)
    stage.send(kv_ref)
    stage.need(wq_ref)
    q_ref[...] = dot(a_ref[own_half(where_ref[0], q_ref.shape[0]), :], wq_ref[...]).astype(BF16)


def project_memory_kernel(stage, memory_ref, wkv_ref, kv_ref):
    stage.need(memory_ref, wkv_ref)
    for at in row_blocks(memory_ref.shape[0]):
        kv_ref[at] = dot(memory_ref[at], wkv_ref[...]).astype(BF16)
    stage.send(kv_ref)


def project_both_kernel(stage, memory_ref, wkv_ref, a_ref, wq_ref, q_ref, kv_ref):
    project_memory_kernel(stage, memory_ref, wkv_ref, kv_ref)
    stage.need(a_ref, wq_ref)
    q_ref[...] = dot(a_ref[...], wq_ref[...]).astype(BF16)


def first_doc(starts_ref, row):
    doc = 0
    for number in range(1, DOCS):
        doc = doc + (starts_ref[0, number] <= row).astype(jnp.int32)
    return doc


def key_range(starts_ref, block_number, causal):
    first = block_number * BLOCK
    low = starts_ref[1, first_doc(starts_ref, first)]
    if causal:
        low = low // BLOCK
        return low * BLOCK, block_number - low
    high = starts_ref[1, first_doc(starts_ref, first + BLOCK - 1) + 1]
    low = low // 128 * 128
    count = (high - low + BLOCK - 1) // BLOCK
    return jnp.minimum(low, starts_ref[1, DOCS] - count * BLOCK), count


def lanes(rows):
    return lax.broadcasted_iota(jnp.int32, (rows, 128), 1)


def causal_mask():
    keys = lax.broadcasted_iota(jnp.int32, (BLOCK, BLOCK), 0)
    rows = lax.broadcasted_iota(jnp.int32, (BLOCK, BLOCK), 1)
    return keys <= rows


def pair_of(ref, pair, rows=slice(None)):
    return ref[rows, pair * 128 : (pair + 1) * 128]


def half_of(head):
    return slice(64 * (head % 2), 64 * (head % 2) + 64)


def in_three(value, place, otherwise):
    high = value.astype(BF16)
    rest = value - high.astype(F32)
    middle = rest.astype(BF16)
    low = (rest - middle.astype(F32)).astype(BF16)
    return jnp.where(place == 4, high, jnp.where(place == 5, middle, jnp.where(place == 6, low, otherwise)))


def walk_keys(starts_ref, block_number, causal, one_block):
    first, count = key_range(starts_ref, block_number, causal)
    if causal:
        one_block(block_number * BLOCK, causal_mask())
    lax.fori_loop(0, count, lambda number, _: (one_block(first + number * BLOCK, None), 0)[1], 0)


def attend_kernel(
    causal, heads, group, stage, where_ref, starts_ref, q_ref, kv_ref, docs_ref, dock_ref, o_ref, qa_ref,
    ka_ref, vt_ref, qs_ref, acc_ref, max_ref,
):
    keys = kv_ref.shape[0]
    pairs = heads // 2
    stage.need(kv_ref, dock_ref)
    left = lanes(keys) < 64
    for pair in range(pairs):
        turned = pair_of(kv_ref, pairs + pair).T
        for head in (2 * pair, 2 * pair + 1):
            mine = left if head % 2 == 0 else ~left
            ka_ref[head] = jnp.where(mine, pair_of(kv_ref, pair), dock_ref[...])
            vt_ref[head, :64] = turned[half_of(head)]
            vt_ref[head, 64:] = jnp.ones((16, keys), BF16)
    left = lanes(BLOCK) < 64
    place = lanes(BLOCK) % 64
    stage.need(q_ref, docs_ref)

    def one_step(step, _):
        at_rows = pl.ds(pl.multiple_of(step * BLOCK, BLOCK), BLOCK)
        block_number = where_ref[0] * (q_ref.shape[0] // BLOCK) + step
        docs = docs_ref[pl.ds(pl.multiple_of(block_number * BLOCK, BLOCK), BLOCK), :]
        for head in range(heads):
            mine = left if head % 2 == 0 else ~left
            scaled = pair_of(q_ref, head // 2, at_rows) * jnp.array(HEAD_DIM**-0.5, BF16)
            qs_ref[head] = jnp.where(mine, scaled, docs)
        max_ref[...] = jnp.full_like(max_ref, LOW)
        acc_ref[...] = jnp.zeros_like(acc_ref)

        def one_block(first_key, mask):
            at = pl.ds(pl.multiple_of(first_key, 128), BLOCK)
            for first in range(0, heads, group):
                some = range(first, first + group)
                scores = [dot_nt(ka_ref[head, at, :], qs_ref[head]) for head in some]
                if mask is not None:
                    scores = [jnp.where(mask, score, LOW) for score in scores]
                old = [max_ref[head, 0:1] for head in some]
                new = [jnp.maximum(m, jnp.max(score, 0, keepdims=True)) for m, score in zip(old, scores)]
                weights = [jnp.exp(score - m).astype(BF16) for score, m in zip(scores, new)]
                mixed = [dot(vt_ref[head, :, at], weight) for head, weight in zip(some, weights)]
                shrink = [jnp.exp(m - n) for m, n in zip(old, new)]
                for number_in, head in enumerate(some):
                    acc_ref[head] = acc_ref[head] * shrink[number_in] + mixed[number_in]
                    max_ref[head, 0:1] = new[number_in]

        walk_keys(starts_ref, block_number, causal, one_block)
        for pair in range(pairs):
            both = []
            for head in (2 * pair, 2 * pair + 1):
                mine = left if head % 2 == 0 else ~left
                acc = acc_ref[head]
                total = acc[64:65]
                both.append(acc[:64] / total)
                lse = max_ref[head, 0:1] + jnp.log(total)
                column = jnp.broadcast_to(-lse, (128, BLOCK)).T
                qa_ref[head, at_rows, :] = jnp.where(mine, qs_ref[head], in_three(column, place, docs))
            o_ref[at_rows, pair * 128 : (pair + 1) * 128] = jnp.concatenate(both, 0).T.astype(BF16)
        return 0

    lax.fori_loop(0, q_ref.shape[0] // BLOCK, one_step, 0)
    stage.send(o_ref, qa_ref)


def attend_back_kernel(
    causal, heads, group, stage, where_ref, starts_ref, qa_ref, kv_ref, do_ref, o_ref, dock_ref, dq_ref, dkv_ref,
    ka_ref, va_ref, da_ref, dqa_ref, dka_ref, dva_ref, kt_ref, qt_ref, dt_ref,
):
    keys = kv_ref.shape[0]
    pairs = heads // 2
    stage.need(kv_ref, dock_ref)
    left = lanes(keys) < 64
    place = lanes(keys) % 64
    ones = jnp.where((place >= 4) & (place < 7), 1.0, 0.0).astype(BF16)
    for head in range(heads):
        mine = left if head % 2 == 0 else ~left
        ka_ref[head] = jnp.where(mine, pair_of(kv_ref, head // 2), dock_ref[...] + ones)
        va_ref[head] = jnp.where(mine, pair_of(kv_ref, pairs + head // 2), ones)
    for pair in range(pairs):
        kt_ref[pair] = pair_of(kv_ref, pair).T
    dka_ref[...] = jnp.zeros_like(dka_ref)
    dva_ref[...] = jnp.zeros_like(dva_ref)
    stage.need(qa_ref, o_ref, do_ref)
    left = lanes(BLOCK) < 64
    place = lanes(BLOCK) % 64

    def one_step(step, _):
        at_rows = pl.ds(pl.multiple_of(step * BLOCK, BLOCK), BLOCK)
        block_number = where_ref[0] * (do_ref.shape[0] // BLOCK) + step
        for pair in range(pairs):
            grad = pair_of(do_ref, pair, at_rows)
            dt_ref[pair] = grad.T
            product = grad.astype(F32) * pair_of(o_ref, pair, at_rows).astype(F32)
            for head in (2 * pair, 2 * pair + 1):
                mine = left if head % 2 == 0 else ~left
                delta = -jnp.sum(jnp.where(mine, product, 0.0), -1, keepdims=True)
                delta = jnp.broadcast_to(delta, (BLOCK, 128))
                da_ref[head] = jnp.where(mine, grad, in_three(delta, place, jnp.zeros((), BF16)))
            qt_ref[pair] = jnp.where(left, qa_ref[2 * pair, at_rows, :], qa_ref[2 * pair + 1, at_rows, :]).T
        dqa_ref[...] = jnp.zeros_like(dqa_ref)

        def one_block(first_key, mask):
            at = pl.ds(pl.multiple_of(first_key, 128), BLOCK)
            for first in range(0, heads, group):
                some = range(first, first + group)
                scores = [dot_nt(ka_ref[head, at, :], qa_ref[head, at_rows, :]) for head in some]
                grads = [dot_nt(va_ref[head, at, :], da_ref[head]) for head in some]
                if mask is not None:
                    scores = [jnp.where(mask, score, LOW) for score in scores]
                weights = [jnp.exp(score) for score in scores]
                grads = [(weight * grad).astype(BF16) for weight, grad in zip(weights, grads)]
                weights = [weight.astype(BF16) for weight in weights]
                values = [dot_nt(dt_ref[head // 2, half_of(head)], weight) for head, weight in zip(some, weights)]
                kept = [dot_nt(qt_ref[head // 2, half_of(head)], grad) for head, grad in zip(some, grads)]
                asked = [dot(kt_ref[head // 2, half_of(head), at], grad) for head, grad in zip(some, grads)]
                for number_in, head in enumerate(some):
                    dva_ref[head // 2, half_of(head), at] += values[number_in]
                    dka_ref[head // 2, half_of(head), at] += kept[number_in]
                    dqa_ref[head // 2, half_of(head)] += asked[number_in]

        walk_keys(starts_ref, block_number, causal, one_block)
        for pair in range(pairs):
            dq_ref[at_rows, pair * 128 : (pair + 1) * 128] = (dqa_ref[pair].T * HEAD_DIM**-0.5).astype(BF16)
        return 0

    lax.fori_loop(0, do_ref.shape[0] // BLOCK, one_step, 0)
    for pair in range(pairs):
        dkv_ref[:, pair * 128 : (pair + 1) * 128] = dka_ref[pair].astype(BF16).T
        dkv_ref[:, (pairs + pair) * 128 : (pairs + pair + 1) * 128] = dva_ref[pair].astype(BF16).T


def out_project(own, other, own_ref, other_ref):
    half = own_ref.shape[1]
    left = dot(own, own_ref[:half]) + dot(other, other_ref[:half])
    right = dot(own, own_ref[half:]) + dot(other, other_ref[half:])
    return jnp.concatenate([left, right], axis=1)


def after_self_kernel(stage, x_ref, own_ref, other_ref, wo_ref, wp_ref, norms_ref, wq_ref, s_ref, a_ref, q_ref):
    stage.need(x_ref, own_ref, wo_ref, wp_ref)
    rows = s_ref.shape[0]
    for at in row_blocks(rows):
        stream = x_ref[at].astype(F32) + out_project(own_ref[at], other_ref[at], wo_ref, wp_ref)
        s_ref[at] = stream
        unit, _ = normalise(stream)
        a_ref[at] = (unit * vector(norms_ref, 2) + vector(norms_ref, 3)).astype(BF16)
    stage.send(s_ref, a_ref)
    stage.need(wq_ref)
    q_ref[...] = dot(a_ref[...], wq_ref[...]).astype(BF16)


def after_cross_kernel(stage, s_ref, own_ref, other_ref, wo_ref, wp_ref, norms_ref, t_ref, a_ref, *parts):
    stage.need(s_ref, own_ref, wo_ref, wp_ref)
    for at in row_blocks(s_ref.shape[0]):
        stream = s_ref[at] + out_project(own_ref[at], other_ref[at], wo_ref, wp_ref)
        t_ref[at] = stream
        unit, _ = normalise(stream)
        a_ref[at] = (unit * vector(norms_ref, 4) + vector(norms_ref, 5)).astype(BF16)
        parts[at.start // BLOCK][...] = a_ref[at]


def prepare_kernel(stage, e_ref, down_ref, memory_ref, wkv_ref, dh_ref, kv_ref):
    stage.need(e_ref, down_ref)
    for at in row_blocks(e_ref.shape[0]):
        dh_ref[at] = dot_nt(e_ref[at], down_ref[...]).astype(BF16)
    stage.send(dh_ref)
    project_memory_kernel(stage, memory_ref, wkv_ref, kv_ref)


def prepare(e, down, memory, wkv):
    rows, width = e.shape
    hidden = down.shape[0]
    return call(
        prepare_kernel,
        (shape((rows, hidden), BF16), shape((memory.shape[0], wkv.shape[1]), BF16)),
        far="FFFF",
        far_out="FF",
        flops=2 * rows * width * hidden,
        scalars=0,
    )(e, down, memory, wkv)


def attend_scratch(heads, keys):
    return [
        pltpu.VMEM((heads, keys, 128), BF16),
        pltpu.VMEM((heads, 80, keys), BF16),
        pltpu.VMEM((heads, BLOCK, 128), BF16),
        pltpu.VMEM((heads, 80, BLOCK), F32),
        pltpu.VMEM((heads, 8, BLOCK), F32),
    ]


def self_own_kernel(heads, stage, side_ref, starts_ref, x, norms, wq, wkv, docs, dock, o, qa, a, kv, q, *scratch):
    norm_project_kernel(stage, side_ref, x, norms, wq, wkv, a, q, kv)
    attend_kernel(True, heads, heads, stage, side_ref, starts_ref, q, kv, docs, dock, o, qa, *scratch)


def self_own(side, starts, x, norms, wq, wkv, docs, dock):
    keys, width = x.shape
    rows, cols = keys // 2, wq.shape[1]
    heads = cols // HEAD_DIM
    return call(
        partial(self_own_kernel, heads),
        (shape((rows, cols), BF16), shape((heads, rows, 128), BF16), shape((keys, width), BF16), shape((keys, 2 * cols), BF16)),
        far="FNFFFF",
        far_out="BFFF",
        flops=5 * keys * width * cols + 16 * rows * keys * cols,
        scalars=2,
        scratch=[pltpu.VMEM((rows, cols), BF16)] + attend_scratch(heads, keys),
    )(side, starts, x, norms, wq, wkv, docs, dock)


def self_other_kernel(
    heads, stage, side_ref, starts_ref, a, wq, wkv, docs, dock, x, own, wo, wp, norms, wc, o, qa, kv, stream, a2, q2, q, *scratch
):
    project_kernel(stage, side_ref, a, wq, wkv, q, kv)
    attend_kernel(True, heads, heads, stage, side_ref, starts_ref, q, kv, docs, dock, o, qa, *scratch)
    after_self_kernel(stage, x, own, o, wo, wp, norms, wc, stream, a2, q2)


def self_other(side, starts, a, wq, wkv, docs, dock, x, own, wo, wp, norms, wc):
    keys, width = a.shape
    rows, cols = own.shape
    heads = cols // HEAD_DIM
    return call(
        partial(self_other_kernel, heads),
        (
            shape((rows, cols), BF16), shape((heads, rows, 128), BF16), shape((keys, 2 * cols), BF16),
            shape((rows, width), F32), shape((rows, width), BF16), shape((rows, cols), BF16),
        ),
        far="FQKFFHNFONF",
        far_out="FFFFFN",
        flops=5 * keys * width * cols + 16 * rows * keys * cols,
        scalars=2,
        scratch=[pltpu.VMEM((rows, cols), BF16)] + attend_scratch(heads, keys),
    )(side, starts, a, wq, wkv, docs, dock, x, own, wo, wp, norms, wc)


def cross_own_kernel(heads, stage, side_ref, starts_ref, kv, q, docs, dock, o, qa, *scratch):
    attend_kernel(False, heads, heads, stage, side_ref, starts_ref, q, kv, docs, dock, o, qa, *scratch)


def cross_own(side, starts, kv, q, docs, dock):
    keys = kv.shape[0]
    rows, cols = q.shape
    heads = cols // HEAD_DIM
    return call(
        partial(cross_own_kernel, heads),
        (shape((rows, cols), BF16), shape((heads, rows, 128), BF16)),
        far="FNFF",
        far_out="BF",
        flops=16 * rows * keys * cols,
        scalars=2,
        scratch=attend_scratch(heads, keys),
    )(side, starts, kv, q, docs, dock)


def cross_other_kernel(
    heads, stage, side_ref, starts_ref, memory, wkv, a, wq, docs, dock, stream, own, wo, wp, norms, o, qa, kv, after, a3, first, second, q, *scratch
):
    project_both_kernel(stage, memory, wkv, a, wq, q, kv)
    attend_kernel(False, heads, heads, stage, side_ref, starts_ref, q, kv, docs, dock, o, qa, *scratch)
    after_cross_kernel(stage, stream, own, o, wo, wp, norms, after, a3, first, second)


def cross_other(side, starts, memory, wkv, a, wq, docs, dock, stream, own, wo, wp, norms):
    keys, width = memory.shape
    rows, cols = own.shape
    heads = cols // HEAD_DIM
    return call(
        partial(cross_other_kernel, heads),
        (
            shape((rows, cols), BF16), shape((heads, rows, 128), BF16), shape((keys, 2 * cols), BF16),
            shape((rows, width), F32), shape((rows, width), BF16), shape((BLOCK, width), BF16), shape((BLOCK, width), BF16),
        ),
        far="FKFQFFFNFON",
        far_out="FFFFNNN",
        flops=5 * keys * width * cols + 16 * rows * keys * cols,
        scalars=2,
        scratch=[pltpu.VMEM((rows, cols), BF16)] + attend_scratch(heads, keys),
    )(side, starts, memory, wkv, a, wq, docs, dock, stream, own, wo, wp, norms)


def feed_kernel(chunk, stage, where_ref, a_ref, dh_ref, up_ref, down_ref, h_ref, du_ref, out_ref, r_ref, *sums):
    rows = a_ref.shape[0]
    out_acc, r_acc = sums if sums else (out_ref, r_ref)
    stage.need(a_ref, up_ref)
    chunks = [slice(first, first + chunk) for first in range(0, up_ref.shape[1], chunk)]
    for some in chunks:
        for at in row_blocks(rows):
            u = dot(a_ref[at], up_ref[:, some])
            if some.start == 0 and at.start == 0:
                stage.need(dh_ref, down_ref)
            square = u * u
            curve = jnp.tanh(u * (0.7978845608028654 + 0.035677408136300125 * square))
            half = 0.5 + 0.5 * curve
            slope = half + (0.5 * u) * (1.0 - curve * curve) * (0.7978845608028654 + 0.10703222440890037 * square)
            h_ref[at, some] = (u * half).astype(BF16)
            du_ref[at, some] = (dh_ref[at, some].astype(F32) * slope).astype(BF16)
        stage.send_columns((h_ref, du_ref), some, some is chunks[-1])
        out_part = dot(h_ref[:, some], down_ref[some])
        if some.start == 0:
            out_acc[...] = out_part
        elif some is chunks[-1]:
            out_ref[...] = (out_acc[...] + out_part).astype(out_ref.dtype)
            stage.send(out_ref)
        else:
            out_acc[...] += out_part
        r_part = dot_nt(du_ref[:, some], up_ref[:, some])
        if some.start == 0:
            r_acc[...] = r_part
        elif some is chunks[-1]:
            r_ref[...] = (r_acc[...] + r_part).astype(r_ref.dtype)
        else:
            r_acc[...] += r_part


def feed(where, a, dh, up, down, dtype, chunk=512):
    rows, width = a.shape
    hidden = up.shape[1]
    return call(
        partial(feed_kernel, chunk),
        (shape((rows, hidden), BF16),) * 2 + (shape((rows, width), dtype),) * 2,
        far="NRFF",
        far_out="FFFN" if dtype == F32 else "FFNN",
        flops=6 * rows * width * hidden,
        limit=24,
        scratch=[] if dtype == F32 else [pltpu.VMEM((rows, width), F32)] * 2,
    )(where, a, dh, up, down)


def grad_into_heads(e, weight_ref):
    half = weight_ref.shape[1]
    return (dot_nt(e[:, :half], weight_ref[:half]) + dot_nt(e[:, half:], weight_ref[half:])).astype(BF16)


def add_rows(ref, number, value):
    ref[number : number + 1, :] += jnp.sum(value, 0, keepdims=True)


def after_feed_kernel(stage, s_ref, r_ref, recv0_ref, recv1_ref, e_ref, norms_ref, wo_ref, wp_ref, g_ref, eb_ref, own_ref, other_ref, d_ref):
    d_ref[...] = jnp.zeros_like(d_ref)
    stage.need(s_ref, r_ref, recv0_ref, recv1_ref, e_ref)
    for at in row_blocks(s_ref.shape[0]):
        unit, rstd = normalise(s_ref[at])
        cotangent = r_ref[at] + (recv0_ref if at.start == 0 else recv1_ref)[...].astype(F32)
        add_rows(d_ref, 0, cotangent * unit)
        add_rows(d_ref, 1, cotangent)
        grad = e_ref[at].astype(F32) + norm_backward(unit, rstd, vector(norms_ref, 4), cotangent)
        g_ref[at] = grad
        eb_ref[at] = grad.astype(BF16)
    stage.send(g_ref, eb_ref)
    stage.need(wo_ref, wp_ref)
    own_ref[...] = grad_into_heads(eb_ref[...], wo_ref)
    other_ref[...] = grad_into_heads(eb_ref[...], wp_ref)


def after_cross_back_kernel(
    stage, s_ref, g_ref, dq_ref, dr_ref, wq_ref, wr_ref, norms_ref, wo_ref, wp_ref, out_ref, eb_ref, own_ref, other_ref, d_ref
):
    d_ref[...] = jnp.zeros_like(d_ref)
    stage.need(s_ref, g_ref, dr_ref, wq_ref, wr_ref)
    for at in row_blocks(s_ref.shape[0]):
        unit, rstd = normalise(s_ref[at])
        cotangent = dot_nt(dq_ref[at], wq_ref[...]) + dot_nt(dr_ref[at], wr_ref[...])
        add_rows(d_ref, 0, cotangent * unit)
        add_rows(d_ref, 1, cotangent)
        grad = g_ref[at] + norm_backward(unit, rstd, vector(norms_ref, 2), cotangent)
        out_ref[at] = grad
        eb_ref[at] = grad.astype(BF16)
    stage.send(out_ref, eb_ref)
    stage.need(wo_ref, wp_ref)
    own_ref[...] = grad_into_heads(eb_ref[...], wo_ref)
    other_ref[...] = grad_into_heads(eb_ref[...], wp_ref)


def key_value_back_kernel(with_queries, stage, where_ref, own_ref, other_ref, wkv_ref, wlw_ref, *refs):
    if with_queries:
        dq_ref, dr_ref, wq_ref, wr_ref, x_ref, send_ref, keep_ref, d_ref = refs
        d_ref[...] = jnp.zeros_like(d_ref)
    else:
        send_ref, keep_ref = refs
    stage.need(own_ref, other_ref, wkv_ref, wlw_ref)
    if with_queries:
        stage.need(x_ref)
    rows = send_ref.shape[0]
    side = where_ref[0]
    for half, target in ((1 - side, send_ref), (side, keep_ref)):
        if with_queries and target is keep_ref:
            stage.need(dq_ref, dr_ref, wq_ref, wr_ref)
        for at in row_blocks(rows):
            place = own_half(half, rows, at.start, BLOCK)
            total = dot_nt(own_ref[place, :], wkv_ref[...]) + dot_nt(other_ref[place, :], wlw_ref[...])
            if with_queries:
                if target is keep_ref:
                    total += dot_nt(dq_ref[at], wq_ref[...]) + dot_nt(dr_ref[at], wr_ref[...])
                unit, _ = normalise(x_ref[place, :].astype(F32))
                add_rows(d_ref, 0, total * unit)
                add_rows(d_ref, 1, total)
            target[at] = total.astype(target.dtype)


def key_value_back(side, own, other, wkv, wlw, queries=()):
    rows = own.shape[0] // 2
    width = wkv.shape[0]
    cols = wkv.shape[1] // 2
    outs = (shape((rows, width), BF16), shape((rows, width), F32))
    if queries:
        outs += (shape((2, width), F32),)
    return call(
        partial(key_value_back_kernel, len(queries) > 0),
        outs,
        far="FFFK",
        far_out="NF",
        flops=18 * rows * width * cols,
    )(side, own, other, wkv, wlw, *queries)


def input_grad_kernel(stage, where_ref, x_ref, g_ref, keep_ref, recv_ref, norms_ref, out_ref):
    stage.need(x_ref, g_ref, keep_ref, recv_ref)
    for at in row_blocks(g_ref.shape[0]):
        unit, rstd = normalise(x_ref[at].astype(F32))
        cotangent = keep_ref[at] + recv_ref[at].astype(F32)
        out_ref[at] = g_ref[at] + norm_backward(unit, rstd, vector(norms_ref, 0), cotangent)


def input_grad(side, x, grad, kept, received, norms):
    rows, width = grad.shape
    return call(
        input_grad_kernel,
        shape((rows, width), F32),
        far="HFF",
        flops=rows * width * 20,
    )(side, x, grad, kept, received, norms)


def bit_reversed(number, bits):
    turned = 0
    for bit in range(bits):
        turned |= ((number >> bit) & 1) << (bits - 1 - bit)
    return turned


def store_parts(product, keep, send, core, parts):
    bits = parts.bit_length() - 1
    rows = product.shape[0] // parts
    product = product.astype(BF16)

    def write(target, wanted):
        for number in range(parts // 2):
            block = bit_reversed(number, bits - 1) * 2 + wanted
            target(number * rows, rows, product[block * rows : (block + 1) * rows])

    for value in (0, 1):
        @pl.when(core == value)
        def _():
            write(keep, value)
            write(send, 1 - value)


def put_columns(ref, columns):
    def put(first, count, value):
        ref[first : first + count, columns] = value

    return put


def attention_grads_kernel(parts, stage, where_ref, wide_ref, a_ref, e_ref, dq_ref, dkv_ref, o_ref, keep_ref, send_ref):
    core = where_ref[1]
    cols = dq_ref.shape[1]
    half = slice(None) if a_ref.shape == e_ref.shape else own_half(where_ref[0], dq_ref.shape[0])
    stage.need(wide_ref, a_ref, e_ref, o_ref)
    products = ((wide_ref, slice(None), dkv_ref, cols), (a_ref, half, dq_ref, 0), (e_ref, slice(None), o_ref, 3 * cols))
    for left, rows, right, first in products:
        product = dot_tn(left[rows, :], right[...])
        columns = slice(first, first + right.shape[1])
        store_parts(product, put_columns(keep_ref, columns), put_columns(send_ref, columns), core, parts)
    stage.send(keep_ref, send_ref)


def feed_grads_kernel(parts, chunk, stage, where_ref, a0, a1, a2, du0, du1, du2, h0, h1, h2, e_ref, keep_ref, send_ref):
    core = where_ref[1]
    rows, hidden = du0.shape
    stage.need(a0, a1, a2, du0, du1, du2)
    stage.fetch(e_ref, h0, h1, h2)
    places = [own_half(where_ref[0], rows)] + [own_half(1 - where_ref[0], rows, at.start, BLOCK) for at in row_blocks(rows)]
    for base in (0, hidden):
        if base > 0:
            stage.need(e_ref, h0, h1, h2)
        for first in range(0, hidden, chunk):
            some = slice(first, first + chunk)
            if base == 0:
                pairs = [(left[...], right[:, some]) for left, right in ((a0, du0), (a1, du1), (a2, du2))]
            else:
                pairs = [(e_ref[place, :], right[:, some]) for place, right in zip(places, (h0, h1, h2))]
            product = dot_tn(*pairs[0]) + dot_tn(*pairs[1]) + dot_tn(*pairs[2])
            columns = slice(base + first, base + first + chunk)
            store_parts(product, put_columns(keep_ref, columns), put_columns(send_ref, columns), core, parts)
            stage.send_columns((keep_ref, send_ref), columns, columns.stop == 2 * hidden)


def attend_back_scratch(heads, keys):
    pairs = heads // 2
    return [
        pltpu.VMEM((heads, keys, 128), BF16),
        pltpu.VMEM((heads, keys, 128), BF16),
        pltpu.VMEM((heads, BLOCK, 128), BF16),
        pltpu.VMEM((pairs, 128, BLOCK), F32),
        pltpu.VMEM((pairs, 128, keys), F32),
        pltpu.VMEM((pairs, 128, keys), F32),
        pltpu.VMEM((pairs, 128, keys), BF16),
        pltpu.VMEM((pairs, 128, BLOCK), BF16),
        pltpu.VMEM((pairs, 128, BLOCK), BF16),
    ]


def after_feed(side, stream, kept, first, second, e3, norms, wo, wp):
    rows, width = stream.shape
    cols = wo.shape[1]
    return call(
        after_feed_kernel_of_side,
        (shape((rows, width), F32), shape((rows, width), BF16), shape((rows, cols), BF16), shape((rows, cols), BF16), shape((2, width), F32)),
        far="FNNNHNFO",
        flops=4 * rows * width * cols,
    )(side, stream, kept, first, second, e3, norms, wo, wp)


def after_feed_kernel_of_side(stage, side_ref, *refs):
    after_feed_kernel(stage, *refs)


def cross_back_kernel(
    parts, heads, stage, where_ref, starts_ref, doo, don, qao, kvo, oo, qan, kvn, on, dock, memory, a2, e2, stream, grad,
    wq, wr, norms, wo, wp,
    keep_d, send_d, keep_c, send_c, dkvo, dkvn, out, e1, own, other, d, dqo, dqn, *scratch
):
    attend_back_kernel(False, heads, heads // 2, stage, where_ref, starts_ref, qao, kvo, doo, oo, dock, dqo, dkvo, *scratch)
    stage.send(dkvo)
    attention_grads_kernel(parts, stage, where_ref, memory, a2, e2, dqo, dkvo, oo, keep_d, send_d)
    attend_back_kernel(False, heads, heads // 2, stage, where_ref, starts_ref, qan, kvn, don, on, dock, dqn, dkvn, *scratch)
    stage.send(dkvn)
    attention_grads_kernel(parts, stage, where_ref, memory, a2, e2, dqn, dkvn, on, keep_c, send_c)
    after_cross_back_kernel(stage, stream, grad, dqn, dqo, wq, wr, norms, wo, wp, out, e1, own, other, d)


def cross_back(where, parts, starts, doo, don, qao, kvo, oo, qan, kvn, on, dock, memory, a2, e2, stream, grad, wq, wr, norms, wo, wp):
    rows, width = stream.shape
    keys, cols = kvo.shape[0], wo.shape[1]
    heads = cols // HEAD_DIM
    part = shape((width // 2, 4 * cols), BF16)
    narrow = shape((rows, cols), BF16)
    return call(
        partial(cross_back_kernel, parts, heads),
        (
            part, part, part, part, shape((keys, 2 * cols), BF16), shape((keys, 2 * cols), BF16), shape((rows, width), F32),
            shape((rows, width), BF16), narrow, narrow, shape((2, width), F32),
        ),
        far="NNFFFFFFFFFNFNFQNFO",
        far_out="FFFFFFFFFNN",
        flops=120 * rows * keys * cols,
        scalars=2,
        limit=44,
        scratch=[pltpu.VMEM((rows, cols), BF16)] * 2 + attend_back_scratch(heads, keys),
    )(where, starts, doo, don, qao, kvo, oo, qan, kvn, on, dock, memory, a2, e2, stream, grad, wq, wr, norms, wo, wp)


def self_other_back_kernel(parts, heads, stage, where_ref, starts_ref, do, qa, kv, o, dock, a1, e1, dq, dkv, keep, send, *scratch):
    attend_back_kernel(True, heads, heads // 2, stage, where_ref, starts_ref, qa, kv, do, o, dock, dq, dkv, *scratch)
    stage.send(dq, dkv)
    attention_grads_kernel(parts, stage, where_ref, a1, a1, e1, dq, dkv, o, keep, send)


def self_other_back(where, parts, starts, do, qa, kv, o, dock, a1, e1):
    rows, cols = do.shape
    keys, width = a1.shape
    heads = cols // HEAD_DIM
    part = shape((width // 2, 4 * cols), BF16)
    return call(
        partial(self_other_back_kernel, parts, heads),
        (shape((rows, cols), BF16), shape((keys, 2 * cols), BF16), part, part),
        far="NFFFFFF",
        far_out="FFFF",
        flops=56 * rows * keys * cols,
        scalars=2,
        limit=34,
        scratch=attend_back_scratch(heads, keys),
    )(where, starts, do, qa, kv, o, dock, a1, e1)


def self_own_back_kernel(
    parts, heads, stage, where_ref, starts_ref, do, qa, kv, o, dock, a1, e1, dqo, dkvo, wkv, wlw, wq, wr, x,
    keep_r, send_r, d, keep, send, dq, dkv, *scratch
):
    attend_back_kernel(True, heads, heads // 2, stage, where_ref, starts_ref, qa, kv, do, o, dock, dq, dkv, *scratch)
    attention_grads_kernel(parts, stage, where_ref, a1, a1, e1, dq, dkv, o, keep, send)
    key_value_back_kernel(True, stage, where_ref, dkv, dkvo, wkv, wlw, dq, dqo, wq, wr, x, send_r, keep_r, d)


def self_own_back(where, parts, starts, do, qa, kv, o, dock, a1, e1, dqo, dkvo, wkv, wlw, wq, wr, x):
    rows, cols = do.shape
    keys, width = a1.shape
    heads = cols // HEAD_DIM
    part = shape((width // 2, 4 * cols), BF16)
    return call(
        partial(self_own_back_kernel, parts, heads),
        (shape((rows, width), F32), shape((rows, width), BF16), shape((2, width), F32), part, part),
        far="FFFFFFFFFFKFQF",
        far_out="FNNFF",
        flops=74 * rows * keys * cols,
        scalars=2,
        limit=36,
        scratch=[pltpu.VMEM((rows, cols), BF16), pltpu.VMEM((keys, 2 * cols), BF16)] + attend_back_scratch(heads, keys),
    )(where, starts, do, qa, kv, o, dock, a1, e1, dqo, dkvo, wkv, wlw, wq, wr, x)


def feed_grads(where, parts, e, a, du, h, chunk=768):
    rows, width = a[0].shape
    hidden = du[0].shape[1]
    out = shape((width // 2, 2 * hidden), BF16)
    return call(
        partial(feed_grads_kernel, parts, chunk),
        (out, out),
        far="NNNFFFLLLL",
        far_out="FF",
        flops=8 * rows * width * hidden,
        limit=30,
    )(where, *a, *du, *h, e)


def swap_tensor(value):
    return lax.ppermute(value, "tensor", [(0, 1), (1, 0)])


def swap_dp(value, bit):
    count = lax.axis_size("dp")
    return lax.ppermute(value, "dp", [(number, number ^ (1 << bit)) for number in range(count)])


def after(value, *others):
    return lax.optimization_barrier((value,) + others)[0] if others else value


def quarter_of(query, key, value, out, part):
    width, cols = query.shape
    rows = width // 4
    pieces = [lax.dynamic_slice_in_dim(weight, part * rows, rows, 0) for weight in (query, key, value)]
    pieces.append(lax.dynamic_slice(out, ((part % 2) * rows, (part // 2) * cols), (rows, cols)))
    return jnp.concatenate(pieces, axis=1)


def whole_of(first, second, third, fourth, part):
    pieces = (first, third, second, fourth)
    return jnp.concatenate([lax.select_n(part ^ number, *pieces) for number in range(4)], axis=0)


class Sum:
    def __init__(self, *terms):
        self.terms = [term if isinstance(term, tuple) else (term, 0) for term in terms]
        last, first = self.terms[-1]
        self.rows = last.shape[0]

    def cut(self, first, rows):
        return Sum.of([(array, start + first) for array, start in self.terms], rows)

    @classmethod
    def of(cls, terms, rows):
        made = cls.__new__(cls)
        made.terms, made.rows = terms, rows
        return made

    def plus(self, array):
        return Sum.of(self.terms + [(array, 0)], self.rows)

    def formed(self, dtype=BF16):
        pieces = [
            array.astype(F32) if array.shape[0] == self.rows else lax.dynamic_slice_in_dim(array, start, self.rows, 0).astype(F32)
            for array, start in self.terms
        ]
        return sum(pieces[1:], pieces[0]).astype(dtype)

    def tied(self, *others):
        arrays = [array for array, _ in self.terms]
        made = lax.optimization_barrier((tuple(arrays), others))
        return (Sum.of([(array, start) for array, (_, start) in zip(made[0], self.terms)], self.rows),) + tuple(made[1])


def halve(value, bit, place):
    rows = value.rows // 2
    mine = (place >> bit) & 1
    return value.cut(mine * rows, rows), swap_dp(value.cut((1 - mine) * rows, rows).formed(), bit)


def add(left, right):
    return (left.astype(F32) + right.astype(F32)).astype(BF16)


def shards(
    target_tokens, memory_tokens, output_grad, target_segments, memory_segments,
    norm1_gain, norm1_shift, self_query, self_key, self_value, self_out,
    norm2_gain, norm2_shift, cross_query, cross_key, cross_value, cross_out,
    norm3_gain, norm3_shift, ffn_up, ffn_down,
):
    _, length, width = target_tokens.shape
    cols = self_query.shape[1]
    parts = lax.axis_size("dp")
    bits = parts.bit_length() - 1
    place = lax.axis_index("dp")
    side = lax.axis_index("tensor")
    core = place & 1
    x = target_tokens[0]
    memory = memory_tokens[0]
    e3 = output_grad[0]
    norms = jnp.stack([norm1_gain, norm1_shift, norm2_gain, norm2_shift, norm3_gain, norm3_shift])
    tie = lax.optimization_barrier
    side_one = side.astype(jnp.int32).reshape(1)
    where = jnp.stack([side, core]).astype(jnp.int32)

    def folded(weight):
        return jnp.concatenate([weight[:, :cols], weight[:, cols:]], axis=0)

    part = place % 4
    self_first = swap_tensor(quarter_of(self_query, self_key, self_value, self_out, part))
    cross_quarter = quarter_of(cross_query, cross_key, cross_value, cross_out, part)
    self_wo = folded(self_out)
    cross_wo = folded(cross_out)
    self_wkv = jnp.concatenate([self_key, self_value], axis=1)
    cross_wkv = jnp.concatenate([cross_key, cross_value], axis=1)

    numbers = jnp.arange(DOCS + 1)[:, None]
    target_starts = jnp.sum(target_segments < numbers, 1).astype(jnp.int32)
    memory_starts = jnp.sum(memory_segments < numbers, 1).astype(jnp.int32)
    self_starts = jnp.stack([target_starts, target_starts])
    cross_starts = jnp.stack([target_starts, memory_starts])
    lane = jnp.arange(128) % 64
    hot = target_segments[0][:, None] == lane[None, :]
    doc_rows = jnp.where(hot, LOW, 0.0).astype(BF16)
    doc_target = jnp.where((lane < DOCS)[None, :] & ~hot, 1.0, 0.0).astype(BF16)
    doc_memory = jnp.where(
        (lane < DOCS)[None, :] & (memory_segments[0][:, None] != lane[None, :]), 1.0, 0.0
    ).astype(BF16)

    dh, kv2_own = prepare(e3, ffn_down, memory, cross_wkv)
    (
        self_first, cross_quarter, x_now, dh, kv2_own, doc_rows, doc_target, doc_memory, self_wo, cross_wo, self_wkv, norms
    ) = tie((self_first, cross_quarter, x, dh, kv2_own, doc_rows, doc_target, doc_memory, self_wo, cross_wo, self_wkv, norms))
    self_second = swap_dp(self_first, 1)
    self_third = swap_dp(self_first, 0)
    cross_first = swap_tensor(cross_quarter)
    o1_own, qa1_own, a1, kv_own, o1_own_far = self_own(
        side_one, self_starts, x_now, norms, self_query, self_wkv, doc_rows, doc_target
    )
    self_second, o1_own, cross_first = tie((self_second, o1_own, cross_first))
    self_fourth = swap_dp(self_second, 0)
    self_fourth, self_third = tie((self_fourth, self_third))
    self_two = whole_of(self_first, self_second, self_third, self_fourth, part)
    cross_first, self_two = tie((cross_first, self_two))
    cross_second = swap_dp(cross_first, 1)
    cross_third = swap_dp(cross_first, 0)
    o1_oth, qa1_oth, kv_oth, stream1, a2, q2_own = self_other(
        side_one, self_starts, a1, self_two, self_two, doc_rows, doc_target, x, o1_own, self_wo, self_two, norms, cross_query
    )
    cross_second, q2_own = tie((cross_second, q2_own))
    cross_fourth = swap_dp(cross_second, 0)
    o2_own, qa2_own, o2_own_far = cross_own(side_one, cross_starts, kv2_own, q2_own, doc_rows, doc_memory)
    cross_fourth, cross_third, o2_own = tie((cross_fourth, cross_third, o2_own))
    cross_two = whole_of(cross_first, cross_second, cross_third, cross_fourth, part)
    o2_oth, qa2_oth, kv2_oth, stream2, a3, a3_first, a3_second = cross_other(
        side_one, cross_starts, memory, cross_two, a2, cross_two, doc_rows, doc_memory, stream1, o2_own, cross_wo, cross_two, norms
    )

    first_block = (side * (length // 2 // BLOCK)).astype(jnp.int32).reshape(1)
    other_block = length // 2 // BLOCK - first_block
    a3_first, a3_second = swap_tensor(a3_first), swap_tensor(a3_second)
    h_own, du_own, out_own, r3_own = feed(first_block, a3, dh, ffn_up, ffn_down, F32)
    a3_first, r3_own = tie((a3_first, r3_own))
    h_first, du_first, out_first, r3_first = feed(other_block, a3_first, dh, ffn_up, ffn_down, BF16)
    a3_second, r3_first = tie((a3_second, r3_first))
    r3_first = swap_tensor(r3_first)
    h_second, du_second, out_second, r3_second = feed(other_block + 1, a3_second, dh, ffn_up, ffn_down, BF16)
    r3_second = swap_tensor(r3_second)
    aligned = (width // parts) % 16 == 0
    static_parts = parts if aligned else 2
    keep_f, send_f = feed_grads(
        where, static_parts, e3, (a3, a3_first, a3_second), (du_own, du_first, du_second), (h_own, h_first, h_second)
    )
    r3_first, r3_second, keep_f, send_f = tie((r3_first, r3_second, keep_f, send_f))

    def reordered(keep, send):
        if aligned:
            return keep, send
        whole = jnp.where(core == 0, jnp.concatenate([keep, send]), jnp.concatenate([send, keep]))
        order = [bit_reversed(number, bits) for number in range(parts)]
        whole = jnp.take(whole.reshape(parts, width // parts, -1), jnp.array(order), axis=0)
        whole = whole.reshape(2, width // 2, -1)
        pick = lambda index: lax.dynamic_index_in_dim(whole, index, 0, False)
        return pick(core), pick(1 - core)

    def swap_core(keep, send):
        keep, send = reordered(keep, send)
        return keep, swap_dp(send, 0)

    keep_f, recv_f = swap_core(keep_f, send_f)
    grad2, e2, do2_own, do2_oth, d3 = after_feed(
        side_one, stream2, r3_own, r3_first, r3_second, e3, norms, cross_wo, cross_two
    )
    do2_oth, keep_f, recv_f, out_first, out_second = tie((do2_oth, keep_f, recv_f, out_first, out_second))
    out_first, out_second = swap_tensor(out_first), swap_tensor(out_second)
    sum_f, recv_f = halve(Sum(keep_f, recv_f), 1, place)
    keep_d, send_d, keep_c, send_c, dkv2_oth, dkv2_own, grad1, e1, do1_own, do1_oth, d2 = cross_back(
        where, static_parts, cross_starts, do2_oth, do2_own, qa2_oth, kv2_oth, o2_oth, qa2_own, kv2_own, o2_own_far,
        doc_memory, memory, a2, e2, stream1, grad2, cross_query, cross_two, norms, self_wo, self_two,
    )
    keep_d, send_d, keep_c, send_c, recv_f, out_first, out_second = tie(
        (keep_d, send_d, keep_c, send_c, recv_f, out_first, out_second)
    )
    keep_d, recv_d = swap_core(keep_d, send_d)
    keep_c, recv_c = swap_core(keep_c, send_c)
    sum_f = sum_f.plus(recv_f)
    send_m, keep_m = key_value_back(side_one, dkv2_own, dkv2_oth, cross_wkv, cross_two)

    do1_oth, keep_d, recv_d, keep_c, recv_c, send_m = tie((do1_oth, keep_d, recv_d, keep_c, recv_c, send_m))
    sum_d, recv_d = halve(Sum(keep_d, recv_d), 1, place)
    recv_m = swap_tensor(send_m)
    dq1_oth, dkv1_oth, keep_t, send_t = self_other_back(
        where, static_parts, self_starts, do1_oth, qa1_oth, kv_oth, o1_oth, doc_target, a1, e1
    )
    keep_t, send_t, recv_d, recv_m = tie((keep_t, send_t, recv_d, recv_m))
    keep_t, recv_t = swap_core(keep_t, send_t)
    do1_own, keep_t, recv_t = tie((do1_own, keep_t, recv_t))
    if bits > 2:
        sum_f, recv_f = halve(sum_f, 2, place)
    sum_t, recv_t = halve(Sum(keep_t, recv_t), 1, place)
    sum_c, recv_c = halve(Sum(keep_c, recv_c), 1, place)
    sent_d = swap_tensor(sum_d.plus(recv_d).formed())
    keep_r, send_r, d1, keep_s, send_s = self_own_back(
        where, static_parts, self_starts, do1_own, qa1_own, kv_own, o1_own_far, doc_target, a1, e1,
        dq1_oth, dkv1_oth, self_wkv, self_two, self_query, self_two, x,
    )
    keep_s, send_s, d1, recv_c, sent_d, recv_t, recv_f = tie((keep_s, send_s, d1, recv_c, sent_d, recv_t, recv_f))
    keep_s, recv_s = swap_core(keep_s, send_s)
    sent_t = swap_tensor(sum_t.plus(recv_t).formed())
    sum_c = sum_c.plus(recv_c).plus(sent_d)
    if bits > 2:
        sum_c, recv_c = halve(sum_c, 2, place)
    lines = jnp.concatenate([jnp.concatenate([d[0:1], d[1:2]], axis=1) for d in (d1, d2, d3)], axis=0)
    lines = jnp.pad(lines, ((0, NORM_ROWS - 3), (0, 0))).astype(BF16)
    lines = add(lines, swap_tensor(lines))
    lines = add(lines, swap_dp(lines, 0))
    keep_s, recv_s, send_r, lines, out_first, out_second = tie((keep_s, recv_s, send_r, lines, out_first, out_second))
    recv_r = swap_tensor(send_r)
    layer_output = (stream2 + out_own + jnp.concatenate([out_first, out_second]).astype(F32)).astype(BF16)
    if bits > 2:
        sum_f = sum_f.plus(recv_f)
    if bits > 3:
        sum_f, recv_f = halve(sum_f, 3, place)
    sum_s = Sum(keep_s, recv_s)

    def halve_with_lines(value, lines, bit):
        rows = value.rows // 2
        mine = (place >> bit) & 1
        message = jnp.concatenate([value.cut((1 - mine) * rows, rows).formed(), lines], axis=0)
        received = swap_dp(message, bit)
        return value.cut(mine * rows, rows).plus(received), add(lines, received[rows:])

    sum_s, lines = halve_with_lines(sum_s, lines, 1)
    sum_s, lines, sent_t, recv_c, recv_f, recv_m, layer_output = sum_s.tied(
        lines, sent_t, recv_c, recv_f, recv_m, layer_output
    )
    sum_s = sum_s.plus(sent_t)
    for bit in range(3, bits):
        sum_f = sum_f.plus(recv_f)
        if bit + 1 < bits:
            sum_f, recv_f = halve(sum_f, bit + 1, place)
    if bits > 2:
        sum_c = sum_c.plus(recv_c)
    for bit in range(3, bits):
        sum_c, recv_c = halve(sum_c, bit, place)
        sum_c = sum_c.plus(recv_c)
    for bit in range(2, bits):
        sum_s, lines = halve_with_lines(sum_s, lines, bit)
        if bit == 2:
            recv_r, lines = tie((recv_r, lines))
    grad_x = input_grad(side_one, x, grad1, keep_r, recv_r, norms)
    grad_memory = keep_m + recv_m.astype(F32)
    small = lines.astype(F32)
    sum_s, sum_c, sum_f = (value.formed(F32) for value in (sum_s, sum_c, sum_f))

    def four(total):
        pieces = [total[:, number * cols : (number + 1) * cols] for number in range(4)]
        return tuple(pieces[:3]) + (pieces[3].T,)

    hidden = ffn_up.shape[1]
    return (
        (layer_output[None], grad_x[None], grad_memory[None])
        + four(sum_s)
        + four(sum_c)
        + (sum_f[:, :hidden], sum_f[:, hidden:].T)
        + tuple(small[number // 2, (number % 2) * width : (number % 2 + 1) * width] for number in range(6))
    )


def solution(mesh):
    tokens = P("dp", None, None)
    columns = P(None, "tensor")
    rows = P("tensor", None)
    block = (P(), P(), columns, columns, columns, rows)
    in_specs = (tokens,) * 3 + (P("dp", None),) * 2 + block + block + (P(), P(), columns, rows)
    out_rows = P("dp", "tensor")
    out_cols = P("tensor", "dp")
    four = (out_rows, out_rows, out_rows, out_cols)
    out_specs = (P("dp", "tensor", None),) * 3 + four + four + (out_rows, out_cols) + (P(),) * 6
    return jax.shard_map(shards, mesh=mesh, in_specs=in_specs, out_specs=out_specs, check_vma=False)
```

time: 346 us -> 295 us (0.85)
  waiting for transfers between devices: 117 us -> 43.9 us
  Pallas kernels: 119 us -> 178 us
  local copies, waits for them, and re-layouts: 35.2 us -> 11.3 us
  starting transfers between devices: 48.3 us -> 24.4 us
  other arithmetic: 18.6 us -> 30.1 us
    pallas_call x26 -> x15, Pallas kernels: 119 us -> 178 us  [run(): pl.pallas_call(wrapped, out_shape=tuple(kept), in_specs=[small] * scalars...]
    ppermute x10 -> x13, waiting for transfers between devices: 64.5 us -> 6.61 us  [swap_tensor(): return lax.ppermute(value, 'tensor', [(0, 1), (1, 0)])]
    unnamed x178 -> x87, local copies, waits for them, and re-layouts: 31.6 us -> 5.04 us
    convert_element_type x1 -> x15, other arithmetic: 1.23 us -> 16.6 us  [the longest x13 15.4 us: formed(): return sum(pieces[1:], pieces[0]).astype(dtype)]
    ppermute x25 -> x23, waiting for transfers between devices: 52.5 us -> 37.3 us  [swap_dp(): lax.ppermute(value, 'dp', [(number, number ^ 1 << bit) for number in rang...]
    ppermute x10 -> x13, starting transfers between devices: 28.5 us -> 14.5 us  [swap_tensor(): return lax.ppermute(value, 'tensor', [(0, 1), (1, 0)])]
    ppermute x25 -> x23, starting transfers between devices: 19.8 us -> 9.82 us  [swap_dp(): lax.ppermute(value, 'dp', [(number, number ^ 1 << bit) for number in rang...]
    convert_element_type x16 -> x4, other arithmetic: 5.43 us -> 0.09 us  [add(): return (left.astype(F32) + right.astype(F32)).astype(BF16)]
  transfers between devices with their start and end apart: 35 -> 36, of which waited for: 18 -> 14; matrix products, arithmetic and copies ran while one was open for 5% -> 9% of each run, Pallas kernels for 25% -> 56%
where the time goes in v1:
time: 295 us; the launch traced here: 289 us
  Pallas kernels  178 us (60%)
  waiting for transfers between devices  43.9 us (15%)
  other arithmetic  30.1 us (10%)
  starting transfers between devices  24.4 us (8%)
  local copies, waits for them, and re-layouts  11.3 us (4%)
    pallas_call x15, Pallas kernels, run(): pl.pallas_call(wrapped, out_shape=tuple(kept), in_specs=[small] * scalars...  178 us
    ppermute x23, waiting for transfers between devices, swap_dp(): lax.ppermute(value, 'dp', [(number, number ^ 1 << bit) for number in rang...  37.3 us
    convert_element_type x13, other arithmetic, formed(): return sum(pieces[1:], pieces[0]).astype(dtype)  15.4 us
    ppermute x13, starting transfers between devices, swap_tensor(): return lax.ppermute(value, 'tensor', [(0, 1), (1, 0)])  14.5 us
    ppermute x23, starting transfers between devices, swap_dp(): lax.ppermute(value, 'dp', [(number, number ^ 1 << bit) for number in rang...  9.82 us
    ppermute x13, waiting for transfers between devices, swap_tensor(): return lax.ppermute(value, 'tensor', [(0, 1), (1, 0)])  6.61 us
  transfers between devices with their start and end apart: 36, of which 14 were waited for; matrix products, arithmetic and copies ran while one was open for 9% of the time, Pallas kernels for 56%

profile of v1, /device:TPU:0, one launch (start us, length us, event | category | flops | bytes accessed | tf_op | source)
XLA Modules:
  0.0 289.3 jit_solution(18358761340495253989)
XLA Ops:
  2.8 3.0 %collective-permute-start = (bf16[192,1536]{1,0:T(8,128)(2,1)S(1)}, bf16[192,1536]{1,0:T(8,128)(2,1)S(1)}, u32[]{:S(2)}, u32[]{:S(2)}) collective-permute-start(bf16[192,1536]{1,0:T(8,128)(2,1)S(1)} %pad_maximum_fusion.4), channel_id=1, source_target_pairs={{0,1},{1,0},{2,3},{3,2},{4,5},{5,4},{6,7},{7,6},{8,9},{9,8},{10,11... | collective-permute-start | bytes 1769480 | tf_op jit(solution)/shard_map/ppermute | solution.py:913
  11.6 7.5 %shard_map.348 = (bf16[1024,1536]{1,0:T(8,128)(2,1)}, bf16[1024,768]{1,0:T(8,128)(2,1)}) custom-call(bf16[1024,768]{1,0:T(8,128)(2,1)} %bitcast.24, bf16[1536,768]{1,0:T(8,128)(2,1)} %refs_4_.7, bf16[1024,768]{1,0:T(8,128)(2,1)} %bitcast.27, bf16[768,768]{1,0:T(8,128)(2,1)} %copy-done.4), custom_call_target="tpu_custom_call" | custom-call | flops 48318384 | bytes 4096 | tf_op jit(solution)/shard_map/pallas_call | solution.py:163
  24.8 10.0 %shard_map.349 = (bf16[512,384]{1,0:T(8,128)(2,1)S(1)}, bf16[6,512,128]{2,1,0:T(8,128)(2,1)}, bf16[1024,768]{1,0:T(8,128)(2,1)}, bf16[1024,768]{1,0:T(8,128)(2,1)}, bf16[512,384]{1,0:T(8,128)(2,1)}) custom-call(s32[1]{0:T(128)} %bitcast.refs_0_, s32[2,5]{1,0:T(2,128)S(1)} %get-tuple-element.347.refs_1_, bf16[1024,768]{1,0:T(8,128)(2,1)} %bitcast.20, ...), custom_call_target="tpu_custom_call" | custom-call | flops 94623496 | bytes 4096 | tf_op jit(solution)/shard_map/pallas_call | solution.py:163
  34.8 2.4 collective-permute-done.1
  38.6 2.1 collective-permute-done.3
  44.2 11.1 %shard_map.350 = (bf16[512,384]{1,0:T(8,128)(2,1)}, bf16[6,512,128]{2,1,0:T(8,128)(2,1)}, bf16[1024,768]{1,0:T(8,128)(2,1)}, f32[512,768]{1,0:T(8,128)}, bf16[51...) custom-call(s32[1]{0:T(128)} %bitcast.refs_0_, s32[2,5]{1,0:T(2,128)S(1)} %get-tuple-element.347.refs_1_, ...), custom_call_target="tpu_custom_call" | custom-call | flops 94623496 | bytes 4096 | tf_op jit(solution)/shard_map/pallas_call | solution.py:163
  55.4 3.7 %collective-permute-done.5 = bf16[192,1536]{1,0:T(8,128)(2,1)S(1)} collective-permute-done((bf16[192,1536]{1,0:T(8,128)(2,1)S(1)}, bf16[192,1536]{1,0:T(8,128)(2,1)S(1)}, u32[]{:S(2)}, u32[]{:S(2)}) %collective-permute-start.5) | collective-permute-done | bytes 589856 | tf_op jit(solution)/shard_map/ppermute | solution.py:918
  59.1 10.7 %shard_map.351 = (bf16[512,384]{1,0:T(8,128)(2,1)S(1)}, bf16[6,512,128]{2,1,0:T(8,128)(2,1)}, bf16[512,384]{1,0:T(8,128)(2,1)}) custom-call(s32[1]{0:T(128)} %bitcast.refs_0_, s32[2,5]{1,0:T(2,128)S(1)} %get-tuple-element.346.refs_1_, bf16[1024,768]{1,0:T(8,128)(2,1)} %get-tuple-element.185.refs_2_.refs_8_, bf16[512,384]{1,0:T(8,128)(2,1)S(1)} %get-tuple-element.186.refs_3_, ...), custom_call_target="tpu_custom_call" | custom-call | flops 64424508 | bytes 4096 | tf_op jit(solution)/shard_map/pallas_call | solution.py:163
  71.6 15.5 %shard_map.352 = (bf16[512,384]{1,0:T(8,128)(2,1)}, bf16[6,512,128]{2,1,0:T(8,128)(2,1)}, bf16[1024,768]{1,0:T(8,128)(2,1)}, f32[512,768]{1,0:T(8,128)}, bf16[51...) custom-call(s32[1]{0:T(128)} %bitcast.refs_0_, s32[2,5]{1,0:T(2,128)S(1)} %get-tuple-element.346.refs_1_, ...), custom_call_target="tpu_custom_call" | custom-call | flops 94623496 | bytes 4096 | tf_op jit(solution)/shard_map/pallas_call | solution.py:163
  87.2 2.0 collective-permute-start.9
  89.2 8.9 %shard_map.353 = (bf16[512,1536]{1,0:T(8,128)(2,1)}, bf16[512,1536]{1,0:T(8,128)(2,1)}, f32[512,768]{1,0:T(8,128)}, f32[512,768]{1,0:T(8,128)S(1)}) custom-call(s32[1]{0:T(128)} %bitcast.9.refs_0_, bf16[512,768]{1,0:T(8,128)(2,1)S(1)} %get-tuple-element.197.refs_1_, bf16[1024,1536]{1,0:T(8,128)(2,1)} %get-tuple-element.198.refs_2_, ...), custom_call_target="tpu_custom_call" | custom-call | flops 72477576 | bytes 4096 | tf_op jit(solution)/shard_map/pallas_call | solution.py:163
  98.8 6.4 %shard_map.354 = (bf16[256,1536]{1,0:T(8,128)(2,1)}, bf16[256,1536]{1,0:T(8,128)(2,1)}, bf16[256,768]{1,0:T(8,128)(2,1)S(1)}, bf16[256,768]{1,0:T(8,128)(2,1)}) custom-call(s32[1]{0:T(128)S(6)} %sub.26.refs_0_, bf16[256,768]{1,0:T(8,128)(2,1)S(1)} %collective-permute-done.8.refs_1_.refs_2_, bf16[1024,1536]{1,0:T(8,128)(2,1)} %get-tuple-element.198.refs_2_, ...), custom_call_target="tpu_custom_call" | custom-call | flops 36238784 | bytes 4096 | tf_op jit(solution)/shard_map/pallas_call | solution.py:163
  105.9 6.4 %shard_map.355 = (bf16[256,1536]{1,0:T(8,128)(2,1)}, bf16[256,1536]{1,0:T(8,128)(2,1)}, bf16[256,768]{1,0:T(8,128)(2,1)S(1)}, bf16[256,768]{1,0:T(8,128)(2,1)}) custom-call(s32[1]{0:T(128)S(6)} %add.335.refs_0_, bf16[256,768]{1,0:T(8,128)(2,1)S(1)} %collective-permute-done.9.refs_1_.refs_3_, bf16[1024,1536]{1,0:T(8,128)(2,1)} %get-tuple-element.198.refs_2_, ...), custom_call_target="tpu_custom_call" | custom-call | flops 36238784 | bytes 4096 | tf_op jit(solution)/shard_map/pallas_call | solution.py:163
  114.6 14.7 %shard_map.356 = (bf16[384,3072]{1,0:T(8,128)(2,1)}, bf16[384,3072]{1,0:T(8,128)(2,1)}) custom-call(s32[2]{0:T(128)S(1)} %pad_add_fusion.2.refs_0_, bf16[512,768]{1,0:T(8,128)(2,1)S(1)} %get-tuple-element.197.refs_1_, bf16[256,768]{1,0:T(8,128)(2,1)S(1)} %collective-permute-done.8.refs_1_.refs_2_, ...), custom_call_target="tpu_custom_call" | custom-call | flops 96636768 | bytes 4096 | tf_op jit(solution)/shard_map/pallas_call | solution.py:163
  129.5 5.4 %shard_map.357 = (f32[512,768]{1,0:T(8,128)S(1)}, bf16[512,768]{1,0:T(8,128)(2,1)S(1)}, bf16[512,384]{1,0:T(8,128)(2,1)S(1)}, bf16[512,384]{1,0:T(8,128)(2,1)S(1)}, f32[2,768]{1,0:T(2,128)S(1)}) custom-call(s32[1]{0:T(128)} %bitcast.refs_0_, f32[512,768]{1,0:T(8,128)} %get-tuple-element.195.refs_1_, f32[512,768]{1,0:T(8,128)S(1)} %get-tuple-element.200.refs_2_, ...), custom_call_target="tpu_custom_call" | custom-call | flops 12079595 | bytes 4096 | tf_op jit(solution)/shard_map/pallas_call | solution.py:163
  138.9 37.5 %shard_map.358 = (bf16[384,1536]{1,0:T(8,128)(2,1)}, bf16[384,1536]{1,0:T(8,128)(2,1)}, bf16[384,1536]{1,0:T(8,128)(2,1)}, bf16[384,1536]{1,0:T(8,128)(2,1)}, bf...) custom-call(s32[2]{0:T(128)S(1)} %pad_add_fusion.2.refs_0_, ...), custom_call_target="tpu_custom_call" | custom-call | flops 483183808 | bytes 4096 | tf_op jit(solution)/shard_map/pallas_call | solution.py:163
  177.1 6.6 %shard_map.359 = (bf16[512,768]{1,0:T(8,128)(2,1)S(1)}, f32[512,768]{1,0:T(8,128)}) custom-call(s32[1]{0:T(128)} %bitcast.refs_0_, bf16[1024,768]{1,0:T(8,128)(2,1)} %get-tuple-element.245.refs_1_, bf16[1024,768]{1,0:T(8,128)(2,1)} %get-tuple-element.246.refs_2_, bf16[768,768]{1,0:T(8,128)(2,1)} %copy-done.4, ...), custom_call_target="tpu_custom_call" | custom-call | flops 54358180 | bytes 4096 | tf_op jit(solution)/shard_map/pallas_call | solution.py:163
  184.1 14.0 %shard_map.360 = (bf16[512,384]{1,0:T(8,128)(2,1)}, bf16[1024,768]{1,0:T(8,128)(2,1)}, bf16[384,1536]{1,0:T(8,128)(2,1)}, bf16[384,1536]{1,0:T(8,128)(2,1)}) custom-call(s32[2]{0:T(128)S(1)} %pad_add_fusion.2.refs_0_, s32[2,5]{1,0:T(2,128)S(1)} %get-tuple-element.347.refs_1_, bf16[512,384]{1,0:T(8,128)(2,1)S(1)} %get-tuple-element.248.refs_2_, ...), custom_call_target="tpu_custom_call" | custom-call | flops 225485776 | bytes 4096 | tf_op jit(solution)/shard_map/pallas_call | solution.py:163
  199.3 4.0 %collective-permute-done.19 = bf16[512,768]{1,0:T(8,128)(2,1)S(1)} collective-permute-done((bf16[512,768]{1,0:T(8,128)(2,1)S(1)}, bf16[512,768]{1,0:T(8,128)(2,1)S(1)}, u32[]{:S(2)}, u32[]{:S(2)}) %collective-permute-start.19) | collective-permute-done | bytes 786464 | tf_op jit(solution)/shard_map/ppermute | solution.py:913
  203.3 2.5 add_convert_fusion.4
  205.7 2.2 add_convert_fusion.7
  209.9 2.1 add_convert_fusion.5
  213.4 18.5 %shard_map.361 = (f32[512,768]{1,0:T(8,128)}, bf16[512,768]{1,0:T(8,128)(2,1)S(1)}, f32[2,768]{1,0:T(2,128)S(1)}, bf16[384,1536]{1,0:T(8,128)(2,1)}, bf16[384,1536]{1,0:T(8,128)(2,1)}) custom-call(s32[2]{0:T(128)S(1)} %pad_add_fusion.2.refs_0_, s32[2,5]{1,0:T(2,128)S(1)} %get-tuple-element.347.refs_1_, bf16[512,384]{1,0:T(8,128)(2,1)} %get-tuple-element.260.refs_2_, ...), custom_call_target="tpu_custom_call" | custom-call | flops 297963360 | bytes 4096 | tf_op jit(solution)/shard_map/pallas_call | solution.py:163
  232.0 4.6 %collective-permute-done.23 = bf16[192,1536]{1,0:T(8,128)(2,1)} collective-permute-done((bf16[192,1536]{1,0:T(8,128)(2,1)}, bf16[192,1536]{1,0:T(8,128)(2,1)}, u32[]{:S(2)}, u32[]{:S(2)}) %collective-permute-start.23) | collective-permute-done | bytes 589856 | tf_op jit(solution)/shard_map/ppermute | solution.py:918
  242.3 1.8 collective-permute-start.30
  246.8 1.8 collective-permute-start.32
  249.8 11.2 %collective-permute-done.28 = bf16[208,1536]{1,0:T(8,128)(2,1)S(1)} collective-permute-done((bf16[208,1536]{1,0:T(8,128)(2,1)S(1)}, bf16[208,1536]{1,0:T(8,128)(2,1)S(1)}, u32[]{:S(2)}, u32[]{:S(2)}) %collective-permute-start.28) | collective-permute-done | bytes 639008 | tf_op jit(solution)/shard_map/ppermute | solution.py:918
  261.0 1.8 collective-permute-done.31
  268.5 5.5 %collective-permute-done.35 = bf16[48,1536]{1,0:T(8,128)(2,1)S(1)} collective-permute-done((bf16[48,1536]{1,0:T(8,128)(2,1)S(1)}, bf16[48,1536]{1,0:T(8,128)(2,1)S(1)}, u32[]{:S(2)}, u32[]{:S(2)}) %collective-permute-start.35) | collective-permute-done | bytes 147488 | tf_op jit(solution)/shard_map/ppermute | solution.py:918
  276.4 2.4 collective-permute-start.34
  279.5 4.5 %shard_map.362 = f32[512,768]{1,0:T(8,128)} custom-call(s32[1]{0:T(128)} %bitcast.refs_0_, bf16[1024,768]{1,0:T(8,128)(2,1)} %bitcast.23, f32[512,768]{1,0:T(8,128)} %get-tuple-element.295.refs_2_, f32[512,768]{1,0:T(8,128)} %get-tuple-element.296.refs_3_, bf16[512,768]{1,0:T(8,128)(2,1)S(1)} %collective-permute-done.32.refs_4_, ...), custom_call_target="tpu_custom_call" | custom-call | flops 157286 | bytes 4096 | tf_op jit(solution)/shard_map/pallas_call | solution.py:163
  284.0 3.6 %collective-permute-done.34 = bf16[64,1536]{1,0:T(8,128)(2,1)S(1)} collective-permute-done((bf16[64,1536]{1,0:T(8,128)(2,1)S(1)}, bf16[64,1536]{1,0:T(8,128)(2,1)S(1)}, u32[]{:S(2)}, u32[]{:S(2)}) %collective-permute-start.34) | collective-permute-done | bytes 196640 | tf_op jit(solution)/shard_map/ppermute | solution.py:918
  (212 shorter events, 53.0 us)
Async XLA Ops:
  2.8 19.6 %collective-permute-start = (bf16[192,1536]{1,0:T(8,128)(2,1)S(1)}, bf16[192,1536]{1,0:T(8,128)(2,1)S(1)}, u32[]{:S(2)}, u32[]{:S(2)}) collective-permute-start(bf16[192,1536]{1,0:T(8,128)(2,1)S(1)} %pad_maximum_fusion.4), channel_id=1, source_target_pairs={{0,1},{1,0},{2,3},{3,2},{4,5},{5,4},{6,7},{7,6},{8,9},{9,8},{10,11... | collective-permute-start | bytes 1769480 | tf_op jit(solution)/shard_map/ppermute | solution.py:913
  22.4 14.8 %collective-permute-start.1 = (bf16[192,1536]{1,0:T(8,128)(2,1)S(1)}, bf16[192,1536]{1,0:T(8,128)(2,1)S(1)}, u32[]{:S(2)}, u32[]{:S(2)}) collective-permute-start(bf16[192,1536]{1,0:T(8,128)(2,1)S(1)} %collective-permute-done), channel_id=1, source_target_pairs={{0,4},{2,6},{4,0},{6,2},{8,12},{10,14},{12,8},{14,10},{16,20},{18,... | collective-permute-start | bytes 1769480 | tf_op jit(solution)/shard_map/ppermute | solution.py:918
  23.9 14.7 %collective-permute-start.2 = (bf16[192,1536]{1,0:T(8,128)(2,1)}, bf16[192,1536]{1,0:T(8,128)(2,1)S(1)}, u32[]{:S(2)}, u32[]{:S(2)}) collective-permute-start(bf16[192,1536]{1,0:T(8,128)(2,1)} %pad_maximum_fusion.5), channel_id=1, source_target_pairs={{0,1},{1,0},{2,3},{3,2},{4,5},{5,4},{6,7},{7,6},{8,9},{9,8},{10,11... | collective-permute-start | bytes 1769480 | tf_op jit(solution)/shard_map/ppermute | solution.py:913
  24.7 13.9 %collective-permute-start.4 = (bf16[192,1536]{1,0:T(8,128)(2,1)S(1)}, bf16[192,1536]{1,0:T(8,128)(2,1)S(1)}, u32[]{:S(2)}, u32[]{:S(2)}) collective-permute-start(bf16[192,1536]{1,0:T(8,128)(2,1)S(1)} %collective-permute-done), channel_id=1, source_target_pairs={{0,2},{2,0},{4,6},{6,4},{8,10},{10,8},{12,14},{14,12},{16,18},{18,... | collective-permute-start | bytes 1769480 | tf_op jit(solution)/shard_map/ppermute | solution.py:918
  43.7 15.4 %collective-permute-start.5 = (bf16[192,1536]{1,0:T(8,128)(2,1)S(1)}, bf16[192,1536]{1,0:T(8,128)(2,1)S(1)}, u32[]{:S(2)}, u32[]{:S(2)}) collective-permute-start(bf16[192,1536]{1,0:T(8,128)(2,1)S(1)} %collective-permute-done.2), channel_id=1, source_target_pairs={{0,4},{2,6},{4,0},{6,2},{8,12},{10,14},{12,8},{14,10},{16,20},{18,... | collective-permute-start | bytes 1769480 | tf_op jit(solution)/shard_map/ppermute | solution.py:918
  44.2 25.5 %collective-permute-start.7 = (bf16[192,1536]{1,0:T(8,128)(2,1)S(1)}, bf16[192,1536]{1,0:T(8,128)(2,1)S(1)}, u32[]{:S(2)}, u32[]{:S(2)}) collective-permute-start(bf16[192,1536]{1,0:T(8,128)(2,1)S(1)} %collective-permute-done.2), channel_id=1, source_target_pairs={{0,2},{2,0},{4,6},{6,4},{8,10},{10,8},{12,14},{14,12},{16,18},{18,... | collective-permute-start | bytes 1769480 | tf_op jit(solution)/shard_map/ppermute | solution.py:918
  59.1 10.7 %collective-permute-start.6 = (bf16[192,1536]{1,0:T(8,128)(2,1)S(1)}, bf16[192,1536]{1,0:T(8,128)(2,1)S(1)}, u32[]{:S(2)}, u32[]{:S(2)}) collective-permute-start(bf16[192,1536]{1,0:T(8,128)(2,1)S(1)} %collective-permute-done.5), channel_id=1, source_target_pairs={{0,2},{2,0},{4,6},{6,4},{8,10},{10,8},{12,14},{14,12},{16,18},{18,... | collective-permute-start | bytes 1769480 | tf_op jit(solution)/shard_map/ppermute | solution.py:918
  87.2 11.7 %collective-permute-start.8 = (bf16[256,768]{1,0:T(8,128)(2,1)}, bf16[256,768]{1,0:T(8,128)(2,1)S(1)}, u32[]{:S(2)}, u32[]{:S(2)}) collective-permute-start(bf16[256,768]{1,0:T(8,128)(2,1)} %get-tuple-element.196), channel_id=1, source_target_pairs={{0,1},{1,0},{2,3},{3,2},{4,5},{5,4},{6,7},{7,6},{8,9},{9,8},{10,11... | collective-permute-start | bytes 1179656 | tf_op jit(solution)/shard_map/ppermute | solution.py:913
  87.2 18.0 %collective-permute-start.9 = (bf16[256,768]{1,0:T(8,128)(2,1)}, bf16[256,768]{1,0:T(8,128)(2,1)S(1)}, u32[]{:S(2)}, u32[]{:S(2)}) collective-permute-start(bf16[256,768]{1,0:T(8,128)(2,1)} %get-tuple-element.201), channel_id=1, source_target_pairs={{0,1},{1,0},{2,3},{3,2},{4,5},{5,4},{6,7},{7,6},{8,9},{9,8},{10,11... | collective-permute-start | bytes 1179656 | tf_op jit(solution)/shard_map/ppermute | solution.py:913
  105.2 24.1 %collective-permute-start.10 = (bf16[256,768]{1,0:T(8,128)(2,1)}, bf16[256,768]{1,0:T(8,128)(2,1)}, u32[]{:S(2)}, u32[]{:S(2)}) collective-permute-start(bf16[256,768]{1,0:T(8,128)(2,1)} %get-tuple-element.204), channel_id=1, source_target_pairs={{0,1},{1,0},{2,3},{3,2},{4,5},{5,4},{6,7},{7,6},{8,9},{9,8},{10,11... | collective-permute-start | bytes 1179656 | tf_op jit(solution)/shard_map/ppermute | solution.py:913
  113.1 16.3 %collective-permute-start.11 = (bf16[256,768]{1,0:T(8,128)(2,1)}, bf16[256,768]{1,0:T(8,128)(2,1)}, u32[]{:S(2)}, u32[]{:S(2)}) collective-permute-start(bf16[256,768]{1,0:T(8,128)(2,1)} %get-tuple-element.206), channel_id=1, source_target_pairs={{0,1},{1,0},{2,3},{3,2},{4,5},{5,4},{6,7},{7,6},{8,9},{9,8},{10,11... | collective-permute-start | bytes 1179656 | tf_op jit(solution)/shard_map/ppermute | solution.py:913
  136.7 39.7 %collective-permute-start.13 = (bf16[192,3072]{1,0:T(8,128)(2,1)S(1)}, bf16[192,3072]{1,0:T(8,128)(2,1)S(1)}, u32[]{:S(2)}, u32[]{:S(2)}) collective-permute-start(bf16[192,3072]{1,0:T(8,128)(2,1)S(1)} %add_convert_fusion), channel_id=1, source_target_pairs={{0,4},{2,6},{4,0},{6,2},{8,12},{10,14},{12,8},{14,10},{16,20},{18,... | collective-permute-start | bytes 3538952 | tf_op jit(solution)/shard_map/ppermute | solution.py:918
  136.8 39.6 %collective-permute-start.14 = (bf16[256,768]{1,0:T(8,128)(2,1)S(1)}, bf16[256,768]{1,0:T(8,128)(2,1)S(1)}, u32[]{:S(2)}, u32[]{:S(2)}) collective-permute-start(bf16[256,768]{1,0:T(8,128)(2,1)S(1)} %copy-done.1), channel_id=1, source_target_pairs={{0,1},{1,0},{2,3},{3,2},{4,5},{5,4},{6,7},{7,6},{8,9},{9,8},{10,11... | collective-permute-start | bytes 1179656 | tf_op jit(solution)/shard_map/ppermute | solution.py:913
  137.4 39.0 %collective-permute-start.15 = (bf16[256,768]{1,0:T(8,128)(2,1)S(1)}, bf16[256,768]{1,0:T(8,128)(2,1)S(1)}, u32[]{:S(2)}, u32[]{:S(2)}) collective-permute-start(bf16[256,768]{1,0:T(8,128)(2,1)S(1)} %copy-done.3), channel_id=1, source_target_pairs={{0,1},{1,0},{2,3},{3,2},{4,5},{5,4},{6,7},{7,6},{8,9},{9,8},{10,11... | collective-permute-start | bytes 1179656 | tf_op jit(solution)/shard_map/ppermute | solution.py:913
  176.4 7.3 %collective-permute-start.16 = (bf16[384,1536]{1,0:T(8,128)(2,1)}, bf16[384,1536]{1,0:T(8,128)(2,1)S(1)}, u32[]{:S(2)}, u32[]{:S(2)}) collective-permute-start(bf16[384,1536]{1,0:T(8,128)(2,1)} %get-tuple-element.242), channel_id=1, source_target_pairs={{0,2},{2,0},{4,6},{6,4},{8,10},{10,8},{12,14},{14,12},{16,18},{18,... | collective-permute-start | bytes 3538952 | tf_op jit(solution)/shard_map/ppermute | solution.py:918
  176.5 7.3 %collective-permute-start.17 = (bf16[384,1536]{1,0:T(8,128)(2,1)}, bf16[384,1536]{1,0:T(8,128)(2,1)S(1)}, u32[]{:S(2)}, u32[]{:S(2)}) collective-permute-start(bf16[384,1536]{1,0:T(8,128)(2,1)} %get-tuple-element.244), channel_id=1, source_target_pairs={{0,2},{2,0},{4,6},{6,4},{8,10},{10,8},{12,14},{14,12},{16,18},{18,... | collective-permute-start | bytes 3538952 | tf_op jit(solution)/shard_map/ppermute | solution.py:918
  183.8 19.5 %collective-permute-start.19 = (bf16[512,768]{1,0:T(8,128)(2,1)S(1)}, bf16[512,768]{1,0:T(8,128)(2,1)S(1)}, u32[]{:S(2)}, u32[]{:S(2)}) collective-permute-start(bf16[512,768]{1,0:T(8,128)(2,1)S(1)} %get-tuple-element.257), channel_id=1, source_target_pairs={{0,1},{1,0},{2,3},{3,2},{4,5},{5,4},{6,7},{7,6},{8,9},{9,8},{10,11... | collective-permute-start | bytes 2359304 | tf_op jit(solution)/shard_map/ppermute | solution.py:913
  184.0 15.2 %collective-permute-start.18 = (bf16[192,1536]{1,0:T(8,128)(2,1)S(1)}, bf16[192,1536]{1,0:T(8,128)(2,1)S(1)}, u32[]{:S(2)}, u32[]{:S(2)}) collective-permute-start(bf16[192,1536]{1,0:T(8,128)(2,1)S(1)} %add_convert_fusion.8), channel_id=1, source_target_pairs={{0,4},{2,6},{4,0},{6,2},{8,12},{10,14},{12,8},{14,10},{16,20},{18,... | collective-permute-start | bytes 1769480 | tf_op jit(solution)/shard_map/ppermute | solution.py:918
  203.2 6.6 %collective-permute-start.20 = (bf16[384,1536]{1,0:T(8,128)(2,1)}, bf16[384,1536]{1,0:T(8,128)(2,1)}, u32[]{:S(2)}, u32[]{:S(2)}) collective-permute-start(bf16[384,1536]{1,0:T(8,128)(2,1)} %get-tuple-element.259), channel_id=1, source_target_pairs={{0,2},{2,0},{4,6},{6,4},{8,10},{10,8},{12,14},{14,12},{16,18},{18,... | collective-permute-start | bytes 3538952 | tf_op jit(solution)/shard_map/ppermute | solution.py:918
  205.7 26.2 %collective-permute-start.24 = (bf16[96,3072]{1,0:T(8,128)(2,1)}, bf16[96,3072]{1,0:T(8,128)(2,1)}, u32[]{:S(2)}, u32[]{:S(2)}) collective-permute-start(bf16[96,3072]{1,0:T(8,128)(2,1)} %add_convert_fusion.4), channel_id=1, source_target_pairs={{0,8},{2,10},{4,12},{6,14},{8,0},{10,2},{12,4},{14,6},{16,24},{18,... | collective-permute-start | bytes 1769480 | tf_op jit(solution)/shard_map/ppermute | solution.py:918
  207.9 24.0 %collective-permute-start.21 = (bf16[192,1536]{1,0:T(8,128)(2,1)}, bf16[192,1536]{1,0:T(8,128)(2,1)}, u32[]{:S(2)}, u32[]{:S(2)}) collective-permute-start(bf16[192,1536]{1,0:T(8,128)(2,1)} %add_convert_fusion.7), channel_id=1, source_target_pairs={{0,4},{2,6},{4,0},{6,2},{8,12},{10,14},{12,8},{14,10},{16,20},{18,... | collective-permute-start | bytes 1769480 | tf_op jit(solution)/shard_map/ppermute | solution.py:918
  209.0 22.9 %collective-permute-start.22 = (bf16[192,1536]{1,0:T(8,128)(2,1)}, bf16[192,1536]{1,0:T(8,128)(2,1)}, u32[]{:S(2)}, u32[]{:S(2)}) collective-permute-start(bf16[192,1536]{1,0:T(8,128)(2,1)} %add_convert_fusion.6), channel_id=1, source_target_pairs={{0,1},{1,0},{2,3},{3,2},{4,5},{5,4},{6,7},{7,6},{8,9},{9,8},{10,11... | collective-permute-start | bytes 1769480 | tf_op jit(solution)/shard_map/ppermute | solution.py:913
  211.9 24.6 %collective-permute-start.23 = (bf16[192,1536]{1,0:T(8,128)(2,1)}, bf16[192,1536]{1,0:T(8,128)(2,1)}, u32[]{:S(2)}, u32[]{:S(2)}) collective-permute-start(bf16[192,1536]{1,0:T(8,128)(2,1)} %add_convert_fusion.5), channel_id=1, source_target_pairs={{0,4},{2,6},{4,0},{6,2},{8,12},{10,14},{12,8},{14,10},{16,20},{18,... | collective-permute-start | bytes 1769480 | tf_op jit(solution)/shard_map/ppermute | solution.py:918
  236.6 7.6 %collective-permute-start.25 = (bf16[384,1536]{1,0:T(8,128)(2,1)}, bf16[384,1536]{1,0:T(8,128)(2,1)S(1)}, u32[]{:S(2)}, u32[]{:S(2)}) collective-permute-start(bf16[384,1536]{1,0:T(8,128)(2,1)} %get-tuple-element.276), channel_id=1, source_target_pairs={{0,2},{2,0},{4,6},{6,4},{8,10},{10,8},{12,14},{14,12},{16,18},{18,... | collective-permute-start | bytes 3538952 | tf_op jit(solution)/shard_map/ppermute | solution.py:918
  238.7 24.1 %collective-permute-start.29 = (bf16[192,1536]{1,0:T(8,128)(2,1)S(1)}, bf16[192,1536]{1,0:T(8,128)(2,1)S(1)}, u32[]{:S(2)}, u32[]{:S(2)}) collective-permute-start(bf16[192,1536]{1,0:T(8,128)(2,1)S(1)} %add_convert_fusion.2), channel_id=1, source_target_pairs={{0,1},{1,0},{2,3},{3,2},{4,5},{5,4},{6,7},{7,6},{8,9},{9,8},{10,11... | collective-permute-start | bytes 1769480 | tf_op jit(solution)/shard_map/ppermute | solution.py:913
  242.3 18.7 %collective-permute-start.30 = (bf16[96,1536]{1,0:T(8,128)(2,1)S(1)}, bf16[96,1536]{1,0:T(8,128)(2,1)S(1)}, u32[]{:S(2)}, u32[]{:S(2)}) collective-permute-start(bf16[96,1536]{1,0:T(8,128)(2,1)S(1)} %add_convert_fusion.11), channel_id=1, source_target_pairs={{0,8},{2,10},{4,12},{6,14},{8,0},{10,2},{12,4},{14,6},{16,24},{18,... | collective-permute-start | bytes 884744 | tf_op jit(solution)/shard_map/ppermute | solution.py:918
  244.4 16.5 %collective-permute-start.28 = (bf16[208,1536]{1,0:T(8,128)(2,1)S(1)}, bf16[208,1536]{1,0:T(8,128)(2,1)S(1)}, u32[]{:S(2)}, u32[]{:S(2)}) collective-permute-start(bf16[208,1536]{1,0:T(8,128)(2,1)S(1)} %pad_maximum_fusion.3), channel_id=1, source_target_pairs={{0,4},{2,6},{4,0},{6,2},{8,12},{10,14},{12,8},{14,10},{16,20},{18,... | collective-permute-start | bytes 1916936 | tf_op jit(solution)/shard_map/ppermute | solution.py:918
  246.7 16.1 %collective-permute-start.31 = (bf16[48,3072]{1,0:T(8,128)(2,1)S(1)}, bf16[48,3072]{1,0:T(8,128)(2,1)S(1)}, u32[]{:S(2)}, u32[]{:S(2)}) collective-permute-start(bf16[48,3072]{1,0:T(8,128)(2,1)S(1)} %add_convert_fusion.10), channel_id=1, source_target_pairs={{0,16},{2,18},{4,20},{6,22},{8,24},{10,26},{12,28},{14,30},{16,0},... | collective-permute-start | bytes 884744 | tf_op jit(solution)/shard_map/ppermute | solution.py:918
  246.8 29.5 %collective-permute-start.32 = (bf16[512,768]{1,0:T(8,128)(2,1)S(1)}, bf16[512,768]{1,0:T(8,128)(2,1)S(1)}, u32[]{:S(2)}, u32[]{:S(2)}) collective-permute-start(bf16[512,768]{1,0:T(8,128)(2,1)S(1)} %get-tuple-element.297), channel_id=1, source_target_pairs={{0,1},{1,0},{2,3},{3,2},{4,5},{5,4},{6,7},{7,6},{8,9},{9,8},{10,11... | collective-permute-start | bytes 2359304 | tf_op jit(solution)/shard_map/ppermute | solution.py:913
  263.0 13.2 %collective-permute-start.33 = (bf16[112,1536]{1,0:T(8,128)(2,1)S(1)}, bf16[112,1536]{1,0:T(8,128)(2,1)S(1)}, u32[]{:S(2)}, u32[]{:S(2)}) collective-permute-start(bf16[112,1536]{1,0:T(8,128)(2,1)S(1)} %pad_maximum_fusion.8), channel_id=1, source_target_pairs={{0,8},{2,10},{4,12},{6,14},{8,0},{10,2},{12,4},{14,6},{16,24},{18,... | collective-permute-start | bytes 1032200 | tf_op jit(solution)/shard_map/ppermute | solution.py:918
  264.2 9.8 %collective-permute-start.35 = (bf16[48,1536]{1,0:T(8,128)(2,1)S(1)}, bf16[48,1536]{1,0:T(8,128)(2,1)S(1)}, u32[]{:S(2)}, u32[]{:S(2)}) collective-permute-start(bf16[48,1536]{1,0:T(8,128)(2,1)S(1)} %add_convert_fusion.12), channel_id=1, source_target_pairs={{0,16},{2,18},{4,20},{6,22},{8,24},{10,26},{12,28},{14,30},{16,0},... | collective-permute-start | bytes 442376 | tf_op jit(solution)/shard_map/ppermute | solution.py:918
  276.4 11.2 %collective-permute-start.34 = (bf16[64,1536]{1,0:T(8,128)(2,1)S(1)}, bf16[64,1536]{1,0:T(8,128)(2,1)S(1)}, u32[]{:S(2)}, u32[]{:S(2)}) collective-permute-start(bf16[64,1536]{1,0:T(8,128)(2,1)S(1)} %pad_maximum_fusion.9), channel_id=1, source_target_pairs={{0,16},{2,18},{4,20},{6,22},{8,24},{10,26},{12,28},{14,30},{16,0},... | collective-permute-start | bytes 589832 | tf_op jit(solution)/shard_map/ppermute | solution.py:918
  (49 other events, 239.9 us)
